TPU v7x, 32 devices: a whole 2x2x4 slice. The times are simulated.
32 devices in a mesh: grp: 4 (over x, core), batch: 2 (over y), mp: 4 (over z).
Axes of the slice: x: 2, y: 2, z: 4, core: 2. Of those that a mesh axis runs over, the one named last changes fastest.
Arguments:
- rows_in: bfloat16 [56, 512, 768], P(('grp', 'batch'), 'mp'), may hold values from -6 to 6
- segment_ids: int32 [56, 512], P(('grp', 'batch')), may hold values from 0 to 3, never falling along the last dimension, each value on 1 to 256 neighbouring positions
- pair_labels: int32 [56, 4], P(('grp', 'batch')), may hold values from 0 to 13
- pair_mask: int32 [56, 4], P(('grp', 'batch')), may hold values 0 or 1
- exit_flag: int32 [56], P(('grp', 'batch')), may hold values from 0 to 1, as said below
- target: int32 [56], P(('grp', 'batch')), may hold values from 0 to 1, as said below
- cot_out: bfloat16 [64, 512, 768], P(('grp', 'batch', 'mp')), may hold values from -6 to 6
- w_qkv: bfloat16 [3, 768, 768], P(None, None, 'mp'), may hold values from -0.21875 to 0.21875
- b_qv: float32 [2, 768], P(None, 'mp'), may hold values from -3 to 3
- w_out: bfloat16 [768, 768], P('mp'), may hold values from -0.625 to 0.625
- b_out: float32 [768], replicated, may hold values from -3 to 3
- ln_gain: float32 [2, 768], replicated, may hold values from 0.25 to 1.75
- ln_bias: float32 [2, 768], replicated, may hold values from -2 to 2
- w_up: bfloat16 [768, 3072], P(None, 'mp'), may hold values from -0.21875 to 0.21875
- b_up: float32 [3072], P('mp'), may hold values from -3 to 3
- w_down: bfloat16 [3072, 768], P('mp'), may hold values from -0.109375 to 0.109375
- b_down: float32 [768], replicated, may hold values from -3 to 3
- s_w1: bfloat16 [768, 128], replicated, may hold values from -0.21875 to 0.21875
- s_bias: float32 [2, 128], replicated, may hold values from -3 to 3
- s_query: float32 [128], replicated, may hold values from -8 to 8
- s_w2: bfloat16 [128, 128], replicated, may hold values from -0.5 to 0.5
- s_w3: bfloat16 [128, 14], replicated, may hold values from -0.5 to 0.5
- s_b3: float32 [14], replicated, may hold values from -3 to 3
Outputs:
- mixed_out: bfloat16 [64, 512, 768], P(('grp', 'batch', 'mp'))
- grad_rows: bfloat16 [56, 512, 768], P(('grp', 'batch'), 'mp')
- g_wqkv: float32 [3, 768, 768], P(None, 'batch', 'mp')
- g_bqv: float32 [2, 768], P(None, ('mp', 'batch'))
- g_wout: float32 [768, 768], P('mp', 'batch')
- g_bout: float32 [768], replicated
- g_lngain: float32 [2, 768], replicated
- g_lnbias: float32 [2, 768], replicated
- g_wup: float32 [768, 3072], P('batch', 'mp')
- g_bup: float32 [3072], P(('mp', 'batch'))
- g_wdown: float32 [3072, 768], P('mp', 'batch')
- g_bdown: float32 [768], replicated
- g_sw1: float32 [768, 128], replicated
- g_sbias: float32 [2, 128], replicated
- g_squery: float32 [128], replicated
- g_sw2: float32 [128, 128], replicated
- g_sw3: float32 [128, 14], replicated
- g_sb3: float32 [14], replicated
Inputs may be any that keep to these rules, and one draw needn't show every extreme that they name: `exit_flag`: 1 marks a row that has exited at an earlier layer. A batch index within the row's own group. Of one device's alive rows at most 4 name the same target, and some device sends exactly 4 to one target; of one group's alive rows at most 8 name the same target, and in every group some target receives exactly 8. `segment_ids`: each of the 4 pairs of a row is one run of positions.
All inputs are finite; a program needn't handle non-finite values. No bound on the sum of `pair_mask` on one device may be relied on, other than what follows from the above.
Results may differ from a plain program's by a relative error of at most 0.028.
Values may be sent and summed in bfloat16 or wider, within the bound.
A program may use at most 192 MiB of HBM per device.

v0:
```python
import jax
import jax.numpy as jnp
from jax import lax
from jax.sharding import PartitionSpec as P

HEAD_DIM = 64


EPS = 1e-12
NEG = -1000000000.0
PRECISE = lax.Precision.HIGHEST


def layer_norm(resid_in, gain_vec, shift_vec):
    center = resid_in - jnp.mean(resid_in, axis=-1, keepdims=True)
    spread = jnp.mean(center * center, axis=-1, keepdims=True)
    return center * lax.rsqrt(spread + EPS) * gain_vec + shift_vec


def gelu_exact(pre_value):
    return jax.nn.gelu(pre_value, approximate=False)


def student_head(hidden, query_vec, w_mid, b_mid, w_cls, b_cls, seg_ids, labels, weights):
    row_total = hidden.shape[0]
    seq_len = hidden.shape[1]
    feat_dim = hidden.shape[2]
    half_dim = feat_dim // 2
    pair_count = labels.shape[-1]
    class_count = b_cls.shape[0]
    head_parts = hidden.reshape(row_total, seq_len, 2, half_dim)
    scores = jnp.einsum(
        "bseh,eh->bse", head_parts, query_vec.reshape(2, half_dim), precision=PRECISE
    ) * half_dim ** (-0.5)
    member = seg_ids[:, None, :] == jnp.arange(pair_count, dtype=jnp.int32)[None, :, None]
    masked = jnp.where(member[:, :, :, None], scores[:, None, :, :], NEG)
    peak_val = jnp.max(masked, axis=2, keepdims=True)
    exp_terms = jnp.exp(masked - peak_val)
    shares = exp_terms / jnp.sum(exp_terms, axis=2, keepdims=True)
    pooled = jnp.einsum("bpse,bseh->bpeh", shares, head_parts, precision=PRECISE).reshape(
        row_total, pair_count, feat_dim
    )
    middle = jnp.tanh(jnp.einsum("bpw,wv->bpv", pooled, w_mid, precision=PRECISE) + b_mid)
    logits = jnp.einsum("bpv,vk->bpk", middle, w_cls, precision=PRECISE) + b_cls
    top_val = jnp.max(logits, axis=-1, keepdims=True)
    log_total = top_val[..., 0] + jnp.log(jnp.sum(jnp.exp(logits - top_val), axis=-1))
    chosen = jnp.sum(
        jnp.where(labels[..., None] == jnp.arange(class_count, dtype=jnp.int32), logits, 0.0),
        axis=-1,
    )
    return jnp.sum(weights * (log_total - chosen))


def score_rows(queries, key_rows, seg_row):
    allowed = seg_row[:, None] == seg_row[None, :]
    scores = jnp.einsum(
        "qhe,khe->hqk", queries, key_rows, preferred_element_type=jnp.float32
    ) * HEAD_DIM ** (-0.5)
    return jnp.where(allowed[None], scores, NEG)


def attend_row(packed):
    queries, key_rows, values, seg_row = packed
    masked = score_rows(queries, key_rows, seg_row)
    top_val = jnp.max(masked, axis=-1, keepdims=True)
    exp_terms = jnp.exp(masked - top_val)
    totals = jnp.sum(exp_terms, axis=-1, keepdims=True)
    prob_low = (exp_terms / totals).astype(jnp.bfloat16)
    context = jnp.einsum("hqk,khe->qhe", prob_low, values, preferred_element_type=jnp.float32)
    return (context, top_val + jnp.log(totals))


def attend_back(packed):
    queries, key_rows, values, seg_row, lse_row, grad_ctx = packed
    probs_full = jnp.exp(score_rows(queries, key_rows, seg_row) - lse_row)
    prob_low = probs_full.astype(jnp.bfloat16)
    grad_prob = jnp.einsum("qhe,khe->hqk", grad_ctx, values, preferred_element_type=jnp.float32)
    grad_values = jnp.einsum("hqk,qhe->khe", prob_low, grad_ctx, preferred_element_type=jnp.float32)
    grad_scores = probs_full * (grad_prob - jnp.sum(probs_full * grad_prob, axis=-1, keepdims=True))
    grad_low = grad_scores.astype(jnp.bfloat16)
    grad_queries = jnp.einsum(
        "hqk,khe->qhe", grad_low, key_rows, preferred_element_type=jnp.float32
    ) * HEAD_DIM ** (-0.5)
    grad_keys = jnp.einsum(
        "hqk,qhe->khe", grad_low, queries, preferred_element_type=jnp.float32
    ) * HEAD_DIM ** (-0.5)
    return jnp.stack([grad_queries, grad_keys, grad_values]).astype(jnp.bfloat16)


def on_device(
    rows_in,
    segment_ids,
    pair_labels,
    pair_mask,
    exit_flag,
    target,
    cot_out,
    w_qkv,
    b_qv,
    w_out,
    b_out,
    ln_gain,
    ln_bias,
    w_up,
    b_up,
    w_down,
    b_down,
    s_w1,
    s_bias,
    s_query,
    s_w2,
    s_w3,
    s_b3,
):
    batch_size = lax.axis_size("batch")
    model_size = lax.axis_size("mp")
    row_count = rows_in.shape[0]
    token_part = rows_in.shape[1]
    model_dim = rows_in.shape[2]
    seq_len = segment_ids.shape[1]
    own_rows = cot_out.shape[0]
    capacity = own_rows * model_size
    slot_depth = (capacity + batch_size - 1) // batch_size
    slot_count = batch_size * slot_depth
    pair_count = pair_labels.shape[1]
    tag_width = 2 * pair_count + 1
    group_dim = w_qkv.shape[2]
    local_heads = group_dim // HEAD_DIM
    alive_rows = 1 - exit_flag > 0
    same_goal = (target[:, None] == target[None, :]) & alive_rows[:, None] & alive_rows[None, :]
    row_order = jnp.arange(row_count, dtype=jnp.int32)
    slot_in = jnp.sum(
        (same_goal & (row_order[None, :] < row_order[:, None])).astype(jnp.int32), axis=1
    )
    flat_slot = target * slot_depth + slot_in
    send_map = (
        (jnp.arange(slot_count, dtype=jnp.int32)[:, None] == flat_slot[None, :])
        & alive_rows[None, :]
    ).astype(jnp.float32)
    send_low = send_map.astype(jnp.bfloat16)
    row_tags = jnp.concatenate(
        [
            pair_labels.astype(jnp.float32),
            pair_mask.astype(jnp.float32),
            jnp.ones((row_count, 1), jnp.float32),
        ],
        axis=1,
    )
    tag_send = (
        jnp.dot(send_map, row_tags, precision=PRECISE)
        .astype(jnp.bfloat16)
        .reshape(batch_size, slot_depth, tag_width)
    )
    seg_send = (
        jnp.dot(send_map, segment_ids.astype(jnp.float32), precision=PRECISE)
        .astype(jnp.bfloat16)
        .reshape(batch_size, slot_depth, seq_len)
    )
    row_send = jnp.einsum(
        "kr,rsd->ksd", send_low, rows_in, preferred_element_type=jnp.float32
    ).astype(jnp.bfloat16)
    row_send = row_send.reshape(batch_size, slot_depth, token_part, model_dim)
    row_got, seg_got, tag_got = (
        lax.all_to_all(row_send, "batch", split_axis=0, concat_axis=0, tiled=True),
        lax.all_to_all(seg_send, "batch", split_axis=0, concat_axis=0, tiled=True),
        lax.all_to_all(tag_send, "batch", split_axis=0, concat_axis=0, tiled=True),
    )
    tag_flat = tag_got.reshape(slot_count, tag_width).astype(jnp.float32)
    live_flat = tag_flat[:, 2 * pair_count]
    position = jnp.cumsum(live_flat.astype(jnp.int32)) - 1
    pick_map = (
        (jnp.arange(capacity, dtype=jnp.int32)[:, None] == position[None, :])
        & (live_flat[None, :] > 0)
    ).astype(jnp.float32)
    pick_low = pick_map.astype(jnp.bfloat16)
    rows_part = jnp.einsum(
        "ck,ksd->csd",
        pick_low,
        row_got.reshape(slot_count, token_part, model_dim),
        preferred_element_type=jnp.float32,
    ).astype(jnp.bfloat16)
    seg_local = jnp.dot(
        pick_map, seg_got.reshape(slot_count, seq_len).astype(jnp.float32), precision=PRECISE
    ).astype(jnp.int32)
    tag_local = jnp.dot(pick_map, tag_flat, precision=PRECISE)
    rows_full = lax.all_gather(rows_part, "mp", axis=1, tiled=True)
    projected = jnp.einsum("csd,jde->jcse", rows_full, w_qkv, preferred_element_type=jnp.float32)
    queries = (
        (projected[0] + b_qv[0])
        .astype(jnp.bfloat16)
        .reshape(capacity, seq_len, local_heads, HEAD_DIM)
    )
    key_rows = projected[1].astype(jnp.bfloat16).reshape(capacity, seq_len, local_heads, HEAD_DIM)
    values = (
        (projected[2] + b_qv[1])
        .astype(jnp.bfloat16)
        .reshape(capacity, seq_len, local_heads, HEAD_DIM)
    )
    context, lse_rows = lax.map(attend_row, (queries, key_rows, values, seg_local))
    context_low = context.astype(jnp.bfloat16).reshape(capacity, seq_len, group_dim)
    attn_part = jnp.einsum("cse,ed->csd", context_low, w_out, preferred_element_type=jnp.float32)
    attn_out = (
        lax.psum_scatter(
            attn_part.astype(jnp.bfloat16), "mp", scatter_dimension=0, tiled=True
        ).astype(jnp.float32)
        + b_out
    )
    first_row = lax.axis_index("mp") * own_rows
    rows_own = lax.dynamic_slice_in_dim(rows_full, first_row, own_rows, 0)
    seg_own = lax.dynamic_slice_in_dim(seg_local, first_row, own_rows, 0)
    tag_own = lax.dynamic_slice_in_dim(tag_local, first_row, own_rows, 0)
    hidden_one, norm_one_back = jax.vjp(
        layer_norm, rows_own.astype(jnp.float32) + attn_out, ln_gain[0], ln_bias[0]
    )
    hidden_low = hidden_one.astype(jnp.bfloat16)
    hidden_all = lax.all_gather(hidden_low, "mp", axis=0, tiled=True)
    pre_act = jnp.einsum("csd,df->csf", hidden_all, w_up, preferred_element_type=jnp.float32) + b_up
    active, gelu_back = jax.vjp(gelu_exact, pre_act)
    active_low = active.astype(jnp.bfloat16)
    down_part = jnp.einsum("csf,fd->csd", active_low, w_down, preferred_element_type=jnp.float32)
    ffn_out = (
        lax.psum_scatter(
            down_part.astype(jnp.bfloat16), "mp", scatter_dimension=0, tiled=True
        ).astype(jnp.float32)
        + b_down
    )
    hidden_two, norm_two_back = jax.vjp(layer_norm, hidden_one + ffn_out, ln_gain[1], ln_bias[1])
    live_own = tag_own[:, 2 * pair_count]
    mixed_out = (hidden_two * live_own[:, None, None]).astype(jnp.bfloat16)
    two_low = hidden_two.astype(jnp.bfloat16)
    student_in = (
        jnp.einsum("csd,dw->csw", two_low, s_w1, preferred_element_type=jnp.float32) + s_bias[0]
    )
    labels_own = tag_own[:, :pair_count].astype(jnp.int32)
    weights_own = tag_own[:, pair_count : 2 * pair_count]

    def head_loss(student_value, query_vec, w_mid, b_mid, w_cls, b_cls):
        return student_head(
            student_value, query_vec, w_mid, b_mid, w_cls, b_cls, seg_own, labels_own, weights_own
        )

    loss_value, head_back = jax.vjp(
        head_loss,
        student_in,
        s_query,
        s_w2.astype(jnp.float32),
        s_bias[1],
        s_w3.astype(jnp.float32),
        s_b3,
    )
    grad_student, g_query, g_mid, g_bmid, g_cls, g_bcls = head_back(jnp.ones((), jnp.float32))
    student_low = grad_student.astype(jnp.bfloat16)
    g_sw1 = jnp.einsum("csd,csw->dw", two_low, student_low, preferred_element_type=jnp.float32)
    g_sb1 = jnp.sum(student_low.astype(jnp.float32), axis=(0, 1))
    grad_two = cot_out.astype(jnp.float32) * live_own[:, None, None]
    grad_two = grad_two + jnp.einsum(
        "csw,dw->csd", student_low, s_w1, preferred_element_type=jnp.float32
    )
    grad_resid_two, g_gain_two, g_shift_two = norm_two_back(grad_two)
    ffn_low = grad_resid_two.astype(jnp.bfloat16)
    g_bdown = jnp.sum(ffn_low.astype(jnp.float32), axis=(0, 1))
    ffn_all = lax.all_gather(ffn_low, "mp", axis=0, tiled=True)
    g_wdown = jnp.einsum("csf,csd->fd", active_low, ffn_all, preferred_element_type=jnp.float32)
    (grad_pre,) = gelu_back(
        jnp.einsum("csd,fd->csf", ffn_all, w_down, preferred_element_type=jnp.float32)
    )
    pre_low = grad_pre.astype(jnp.bfloat16)
    g_bup = jnp.sum(pre_low.astype(jnp.float32), axis=(0, 1))
    g_wup = jnp.einsum("csd,csf->df", hidden_all, pre_low, preferred_element_type=jnp.float32)
    up_part = jnp.einsum("csf,df->csd", pre_low, w_up, preferred_element_type=jnp.float32)
    grad_one = grad_resid_two + lax.psum_scatter(
        up_part.astype(jnp.bfloat16), "mp", scatter_dimension=0, tiled=True
    ).astype(jnp.float32)
    grad_resid_one, g_gain_one, g_shift_one = norm_one_back(grad_one)
    attn_low = grad_resid_one.astype(jnp.bfloat16)
    g_bout = jnp.sum(attn_low.astype(jnp.float32), axis=(0, 1))
    attn_all = lax.all_gather(attn_low, "mp", axis=0, tiled=True)
    g_wout = jnp.einsum("cse,csd->ed", context_low, attn_all, preferred_element_type=jnp.float32)
    grad_context = jnp.einsum(
        "csd,ed->cse", attn_all, w_out, preferred_element_type=jnp.float32
    ).astype(jnp.bfloat16)
    grad_context = grad_context.reshape(capacity, seq_len, local_heads, HEAD_DIM)
    grad_proj = lax.map(attend_back, (queries, key_rows, values, seg_local, lse_rows, grad_context))
    grad_proj = grad_proj.reshape(capacity, 3, seq_len, group_dim)
    g_bqv = jnp.stack(
        [
            jnp.sum(grad_proj[:, 0].astype(jnp.float32), axis=(0, 1)),
            jnp.sum(grad_proj[:, 2].astype(jnp.float32), axis=(0, 1)),
        ]
    )
    g_wqkv = jnp.einsum("cjse,csd->jde", grad_proj, rows_full, preferred_element_type=jnp.float32)
    grad_input = jnp.einsum("cjse,jde->csd", grad_proj, w_qkv, preferred_element_type=jnp.float32)
    resid_rows = lax.dynamic_slice_in_dim(grad_input, first_row, own_rows, 0) + grad_resid_one
    grad_input = lax.dynamic_update_slice_in_dim(grad_input, resid_rows, first_row, 0)
    grad_mine = lax.psum_scatter(
        grad_input.astype(jnp.bfloat16), "mp", scatter_dimension=1, tiled=True
    )
    back_send = jnp.einsum(
        "ck,csd->ksd", pick_low, grad_mine, preferred_element_type=jnp.float32
    ).astype(jnp.bfloat16)
    back_send = back_send.reshape(batch_size, slot_depth, token_part, model_dim)
    back_got = lax.all_to_all(back_send, "batch", split_axis=0, concat_axis=0, tiled=True)
    grad_rows = jnp.einsum(
        "kr,ksd->rsd",
        send_low,
        back_got.reshape(slot_count, token_part, model_dim),
        preferred_element_type=jnp.float32,
    ).astype(jnp.bfloat16)
    matrix_grads = (
        lax.psum_scatter(
            g_wqkv.astype(jnp.bfloat16), "batch", scatter_dimension=1, tiled=True
        ).astype(jnp.float32),
        lax.psum_scatter(
            g_bqv.astype(jnp.bfloat16), "batch", scatter_dimension=1, tiled=True
        ).astype(jnp.float32),
        lax.psum_scatter(
            g_wout.astype(jnp.bfloat16), "batch", scatter_dimension=1, tiled=True
        ).astype(jnp.float32),
        lax.psum_scatter(
            g_wup.astype(jnp.bfloat16), "batch", scatter_dimension=0, tiled=True
        ).astype(jnp.float32),
        lax.psum_scatter(
            g_bup.astype(jnp.bfloat16), "batch", scatter_dimension=0, tiled=True
        ).astype(jnp.float32),
        lax.psum_scatter(
            g_wdown.astype(jnp.bfloat16), "batch", scatter_dimension=1, tiled=True
        ).astype(jnp.float32),
    )
    matrix_grads = (
        lax.psum(matrix_grads[0].astype(jnp.bfloat16), "grp").astype(jnp.float32),
        lax.psum(matrix_grads[1].astype(jnp.bfloat16), "grp").astype(jnp.float32),
        lax.psum(matrix_grads[2].astype(jnp.bfloat16), "grp").astype(jnp.float32),
        lax.psum(matrix_grads[3].astype(jnp.bfloat16), "grp").astype(jnp.float32),
        lax.psum(matrix_grads[4].astype(jnp.bfloat16), "grp").astype(jnp.float32),
        lax.psum(matrix_grads[5].astype(jnp.bfloat16), "grp").astype(jnp.float32),
    )
    small_grads = lax.psum(
        (
            g_bout,
            jnp.stack([g_gain_one, g_gain_two]),
            jnp.stack([g_shift_one, g_shift_two]),
            g_bdown,
            g_sw1,
            jnp.stack([g_sb1, g_bmid]),
            g_query,
            g_mid,
            g_cls,
            g_bcls,
        ),
        ("grp", "batch", "mp"),
    )
    return (
        mixed_out,
        grad_rows,
        matrix_grads[0],
        matrix_grads[1],
        matrix_grads[2],
        small_grads[0],
        small_grads[1],
        small_grads[2],
        matrix_grads[3],
        matrix_grads[4],
        matrix_grads[5],
        small_grads[3],
        small_grads[4],
        small_grads[5],
        small_grads[6],
        small_grads[7],
        small_grads[8],
        small_grads[9],
    )


def solution(mesh):
    return jax.shard_map(
        on_device,
        mesh=mesh,
        in_specs=(
            P(("grp", "batch"), "mp", None),
            P(("grp", "batch"), None),
            P(("grp", "batch"), None),
            P(("grp", "batch"), None),
            P(("grp", "batch")),
            P(("grp", "batch")),
            P(("grp", "batch", "mp"), None, None),
            P(None, None, "mp"),
            P(None, "mp"),
            P("mp", None),
            P(),
            P(),
            P(),
            P(None, "mp"),
            P("mp"),
            P("mp", None),
            P(),
            P(),
            P(),
            P(),
            P(),
            P(),
            P(),
        ),
        out_specs=(
            P(("grp", "batch", "mp"), None, None),
            P(("grp", "batch"), "mp", None),
            P(None, "batch", "mp"),
            P(None, ("mp", "batch")),
            P("mp", "batch"),
            P(),
            P(),
            P(),
            P("batch", "mp"),
            P(("mp", "batch")),
            P("mp", "batch"),
            P(),
            P(),
            P(),
            P(),
            P(),
            P(),
            P(),
        ),
        check_vma=False,
    )
```

profile of v0, /device:TPU:1, one launch (start us, length us, event | category | flops | bytes accessed | tf_op | source)
XLA Modules:
  0.0 1486.8 jit_solution(14273637690790820167)
XLA Ops:
  11.8 3.3 all-to-all-start
  15.2 2.2 convolution_convert_fusion.6
  17.4 2.9 reshape.387
  22.0 3.7 all-to-all-start.1
  26.1 18.9 %all-to-all-done.1 = bf16[2,4,128,768]{3,1,2,0:T(4,128)(2,1)S(1)} async-done(((bf16[2,4,128,768]{3,1,2,0:T(4,128)(2,1)}), bf16[2,4,128,768]{3,1,2,0:T(4,128)(2,1)S(1)}, u32[]{:S(2)}, u32[]{:S(2)}) %all-to-all-start.1) | async-done | bytes 1572896 | tf_op jit(solution)/shard_map/all_to_all | solution.py:164
  46.7 2.7 reshape.388
  52.3 3.2 all-to-all-start.2
  58.5 109.8 %all-gather.5.cloned.1.call-done = bf16[8,512,768]{2,0,1:T(8,128)(2,1)} async-done(((bf16[8,128,768]{2,0,1:T(8,128)(2,1)}), bf16[8,512,768]{2,0,1:T(8,128)(2,1)}) %all-gather.5.cloned.1.call-update) | async-done | bytes 6291472 | tf_op jit(solution)/shard_map/all_gather | solution.py:186
  168.3 6.3 fusion.56
  175.8 2.8 add_convert_fusion.1
  178.6 42.9 %while.22 = (s32[]{:T(128)}, bf16[8,512,3,64]{1,3,2,0:T(8,128)(2,1)}, f32[8,3,512,1]{2,1,3,0:T(4,128)S(1)}, bf16[8,512,3,64]{1,3,2,0:T(8,128)(2,1)}, s32[8,512]{...) while((s32[]{:T(128)}, ...), condition=%wide.region_5.6_spmd, body=%wide.region_2.5_spmd.sunk | while | flops 211024384 | bytes 11532381 | solution.py:199
  181.3 2.7 fusion.217
  186.6 2.7 fusion.217
  192.0 2.7 fusion.217
  197.3 2.7 fusion.217
  202.7 2.7 fusion.217
  208.1 2.7 fusion.217
  213.4 2.7 fusion.217
  218.8 2.7 fusion.217
  221.5 6.5 convolution_convert_fusion
  228.8 4.4 constant_dynamic-slice_fusion.4
  233.2 103.8 %reduce-scatter.18.cloned.1.call-done = bf16[2,512,768]{2,1,0:T(8,128)(2,1)} async-done(((bf16[8,512,768]{2,1,0:T(8,128)(2,1)}), bf16[2,512,768]{2,1,0:T(8,128)(2,1)}) %reduce-scatter.18.cloned.1.call-update) | async-done | bytes 1572880 | tf_op jit(solution)/shard_map/reduce_scatter | solution.py:203
  342.0 116.2 %all-gather.7.cloned.1.call-done = bf16[8,512,768]{2,1,0:T(8,128)(2,1)} async-done(((bf16[2,512,768]{2,1,0:T(8,128)(2,1)}), bf16[8,512,768]{2,1,0:T(8,128)(2,1)}) %all-gather.7.cloned.1.call-update) | async-done | bytes 6291472 | tf_op jit(solution)/shard_map/all_gather | solution.py:216
  458.1 11.1 fusion.60
  469.3 29.9 %multiply_convert_fusion.1 = (bf16[8,512,768]{2,1,0:T(8,128)(2,1)S(1)}, f32[8,512,768]{2,1,0:T(8,128)}) fusion(f32[8,512,768]{2,1,0:T(8,128)S(1)} %get-tuple-element.269, f32[768]{0:T(1024)S(1)} %copy-done.24, u8[512,768]{1,0:T(8,128)(4,1)S(1)} %get-tuple-element.174, u8[512,768]{1,0:T(8,128)(4,1)S(1)} %get-tuple-element.173), kind=kLoop, calls=%fused_computation.67 | loop fusion | flops 223346688 | bytes 32246784 | tf_op jit(solution)/shard_map/convert_element_type | solution.py:219
  499.1 2.6 copy-done.11
  501.7 7.0 convolution_convert_fusion.2
  510.0 107.7 %reduce-scatter.20.cloned.1.call-done = bf16[2,512,768]{2,1,0:T(8,128)(2,1)} async-done(((bf16[8,512,768]{2,1,0:T(8,128)(2,1)}), bf16[2,512,768]{2,1,0:T(8,128)(2,1)}) %reduce-scatter.20.cloned.1.call-update) | async-done | bytes 1572880 | tf_op jit(solution)/shard_map/reduce_scatter | solution.py:222
  617.7 2.9 fusion.159
  627.1 3.6 multiply_reduce_fusion.1
  630.8 2.5 fusion.156
  636.6 116.0 %all-gather.9.cloned.1.call-done = bf16[8,512,768]{2,1,0:T(8,128)(2,1)} async-done(((bf16[2,512,768]{2,1,0:T(8,128)(2,1)}), bf16[8,512,768]{2,1,0:T(8,128)(2,1)}) %all-gather.9.cloned.1.call-update) | async-done | bytes 6291472 | tf_op jit(solution)/shard_map/all_gather | solution.py:262
  752.6 16.8 %fusion.163 = (bf16[768]{0:T(1024)(128)(2,1)S(1)}, bf16[8,512,768]{2,1,0:T(8,128)(2,1)}) fusion(f32[8,512,768]{2,1,0:T(8,128)} %get-tuple-element.254, bf16[8,512,768]{2,1,0:T(8,128)(2,1)} %all-gather.9.cloned.1.call-done, bf16[768,768]{1,0:T(8,128)(2,1)} %param.42, f32[8,512,768]{2,1,0:T(8,128)} %copy-done.10, f32[768]{0:T(1024)S(1)} %copy-done.24), kind=kOutput, calls=%fused_computation.281 | convolution fusion | flops 4882168832 | bytes 38932992 | tf_op jit(solution)/shard_map/csd,fd->csf/dot_general | solution.py:265
  769.4 9.7 convolution_convert_fusion.1
  779.2 108.9 %reduce-scatter.22.cloned.1.call-done = bf16[2,512,768]{2,1,0:T(8,128)(2,1)} async-done(((bf16[8,512,768]{2,1,0:T(8,128)(2,1)}), bf16[2,512,768]{2,1,0:T(8,128)(2,1)}) %reduce-scatter.22.cloned.1.call-update) | async-done | bytes 1572880 | tf_op jit(solution)/shard_map/reduce_scatter | solution.py:271
  888.1 3.9 multiply_reduce_fusion.2
  892.4 3.2 fusion.155
  898.8 9.1 bitcast_convert_fusion
  909.6 105.3 %all-gather.11.cloned.1.call-done = bf16[8,512,768]{2,1,0:T(8,128)(2,1)} async-done(((bf16[2,512,768]{2,1,0:T(8,128)(2,1)}), bf16[8,512,768]{2,1,0:T(8,128)(2,1)}) %all-gather.11.cloned.1.call-update) | async-done | bytes 6291472 | tf_op jit(solution)/shard_map/all_gather | solution.py:277
  1014.9 5.0 convolution_convert_fusion.7
  1019.9 73.3 %while.23 = (s32[]{:T(128)}, bf16[8,3,512,3,64]{2,4,3,1,0:T(8,128)(2,1)}, bf16[8,512,3,64]{1,3,2,0:T(8,128)(2,1)}, s32[8,512]{1,0:T(8,128)S(1)}, bf16[8,512,3,64...) while((s32[]{:T(128)}, ...), condition=%wide.region_29.30_spmd, body=%wide.region_27.29_spmd.sunk | while | flops 512915968 | bytes 27303528 | solution.py:283
  1021.7 2.3 multiply_reduce_fusion.9
  1031.0 2.2 multiply_reduce_fusion.9
  1093.2 4.7 fusion.69
  1098.8 9.2 copy.151
  1108.1 9.5 fusion.67
  1117.5 2.5 copy.182
  1120.1 2.3 reshape.428
  1122.8 9.9 bitcast_convert_fusion.1
  1132.8 10.4 convolution_bitcast_fusion
  1143.2 4.0 add_dynamic-update-slice_fusion
  1147.2 8.3 convert_element_type.258
  1155.6 2.4 slice_reduce_fusion.1
  1167.8 111.4 %reduce-scatter.24.cloned.1.call-done = bf16[8,128,768]{2,1,0:T(8,128)(2,1)} async-done(((bf16[8,512,768]{2,1,0:T(8,128)(2,1)}), bf16[8,128,768]{2,1,0:T(8,128)(2,1)}) %reduce-scatter.24.cloned.1.call-update) | async-done | bytes 1572880 | tf_op jit(solution)/shard_map/reduce_scatter | solution.py:295
  1279.2 2.4 convolution_convert_fusion.4
  1283.0 3.1 copy.149
  1286.1 3.7 all-to-all-start.3
  1290.9 3.7 convolution_bitcast_fusion.3
  1294.9 13.8 all-reduce
  1308.8 41.0 %all-reduce.1 = (f32[768]{0:T(1024)}, f32[2,768]{1,0:T(2,128)}, f32[2,768]{1,0:T(2,128)}, f32[768]{0:T(1024)}, f32[2,128]{1,0:T(2,128)}, /*index=5*/f32[128]{0:T(128)}, f32[128,14]{0,1:T(8,128)}, f32[14]{0:T(128)}) all-reduce(f32[768]{0:T(1024)S(1)} %get-tuple-element.243, ...), channel_id=1, replica_groups=mesh['grp'=4,'batch'=2,'mp'=4] {'grp','batch','mp'}, use_global_device_ids=true, to_apply=%region_40.41 | all-reduce | flops 6798 | bytes 54384 | tf_op jit(solution)/shard_map/psum | solution.py:337
  1350.6 7.3 all-reduce.3
  1359.1 2.2 convert_element_type.271
  1366.8 2.9 reshape.399
  1371.7 105.2 %all-reduce.8.cloned.1.call-done = (f32[768,128]{1,0:T(8,128)}, f32[128,128]{1,0:T(8,128)}) async-done(((f32[768,128]{1,0:T(8,128)}, f32[128,128]{1,0:T(8,128)}), (f32[768,128]{1,0:T(8,128)}, f32[128,128]{1,0:T(8,128)})) %all-reduce.8.cloned.1.call-update) | async-done | bytes 458768 | tf_op jit(solution)/shard_map/psum | solution.py:337
  (343 shorter events, 153.0 us)
Async XLA Ops:
  7.2 8.0 copy-start
  8.0 43.4 %copy-start.19 = (pred[7]{0:T(512)(128)(4,1)}, pred[7]{0:T(512)(128)(4,1)S(1)}, u32[]{:S(2)}) copy-start(pred[7]{0:T(512)(128)(4,1)S(1)} %subtract_compare_fusion) | copy-start | bytes 25
  9.6 41.9 %copy-start.25 = (s32[7]{0:T(128)}, s32[7]{0:T(128)S(1)}, u32[]{:S(2)}) copy-start(s32[7]{0:T(128)S(1)} %multiply_add_fusion.5) | copy-start | bytes 88
  11.8 10.1 all-to-all-start
  22.0 23.1 %all-to-all-start.1 = ((bf16[2,4,128,768]{3,1,2,0:T(4,128)(2,1)}), bf16[2,4,128,768]{3,1,2,0:T(4,128)(2,1)S(1)}, u32[]{:S(2)}, u32[]{:S(2)}) async-start(bf16[2,4,128,768]{3,1,2,0:T(4,128)(2,1)} %copy.139), calls=%async_computation.1 | async-start | bytes 3145728 | tf_op jit(solution)/shard_map/all_to_all | solution.py:164
  25.6 142.6 %all-gather.5.cloned.1.call-start = ((), (), s32[]{:S(2)}) async-start(), calls=%async_computation.13 | async-start | bytes 7864320 | tf_op jit(solution)/shard_map/all_gather | solution.py:186
  49.5 2.0 copy-start.35
  49.5 6.4 copy-start.27
  49.5 118.8 %copy-start.32 = (bf16[3,768,192]{1,2,0:T(8,128)(2,1)S(1)}, bf16[3,768,192]{1,2,0:T(8,128)(2,1)}, u32[]{:S(2)}) copy-start(bf16[3,768,192]{1,2,0:T(8,128)(2,1)} %param.34) | copy-start | bytes 2654212
  52.3 5.9 all-to-all-start.2
  55.6 281.4 %reduce-scatter.18.cloned.1.call-start = ((), (), s32[]{:S(2)}) async-start(), calls=%async_computation.14 | async-start | bytes 7864320 | tf_op jit(solution)/shard_map/reduce_scatter | solution.py:203
  178.6 42.9 %copy-start.14 = (bf16[192,768]{1,0:T(8,128)(2,1)S(1)}, bf16[192,768]{1,0:T(8,128)(2,1)}, u32[]{:S(2)}) copy-start(bf16[192,768]{1,0:T(8,128)(2,1)} %param.36) | copy-start | bytes 884740
  221.5 6.5 copy-start.9
  228.0 0.7 copy-start.21
  228.0 0.7 copy-start.22
  228.0 109.0 %copy-start.16 = (f32[768]{0:T(1024)S(1)}, f32[768]{0:T(1024)}, u32[]{:S(2)}) copy-start(f32[768]{0:T(1024)} %param.37) | copy-start | bytes 9220
  228.1 230.1 %all-gather.7.cloned.1.call-start = ((), (), s32[]{:S(2)}) async-start(), calls=%async_computation.15 | async-start | bytes 7864320 | tf_op jit(solution)/shard_map/all_gather | solution.py:216
  337.0 2.0 copy-start.2
  339.9 118.2 %copy-start.24 = (f32[768]{0:T(1024)S(1)}, f32[768]{0:T(1024)}, u32[]{:S(2)}) copy-start(f32[768]{0:T(1024)} %param.41) | copy-start | bytes 9220
  341.9 275.8 %reduce-scatter.20.cloned.1.call-start = ((), (), s32[]{:S(2)}) async-start(), calls=%async_computation.16 | async-start | bytes 7864320 | tf_op jit(solution)/shard_map/reduce_scatter | solution.py:222
  469.2 29.9 %copy-start.10 = (f32[8,512,768]{2,1,0:T(8,128)}, f32[8,512,768]{2,1,0:T(8,128)S(1)}, u32[]{:S(2)}) copy-start(f32[8,512,768]{2,1,0:T(8,128)S(1)} %get-tuple-element.269) | copy-start | bytes 37748740
  469.2 32.5 %copy-start.30 = (bf16[768,768]{1,0:T(8,128)(2,1)S(1)}, bf16[768,768]{1,0:T(8,128)(2,1)}, u32[]{:S(2)}) copy-start(bf16[768,768]{1,0:T(8,128)(2,1)} %param.42) | copy-start | bytes 3538948
  499.1 2.6 copy-start.11
  508.7 0.7 copy-start.36
  508.7 0.8 copy-start.28
  508.7 109.0 %copy-start.23 = (f32[768]{0:T(1024)S(1)}, f32[768]{0:T(1024)}, u32[]{:S(2)}) copy-start(f32[768]{0:T(1024)} %param.43) | copy-start | bytes 9220
  508.7 243.9 %all-gather.9.cloned.1.call-start = ((), (), s32[]{:S(2)}) async-start(), calls=%async_computation.17 | async-start | bytes 7864320 | tf_op jit(solution)/shard_map/all_gather | solution.py:262
  620.6 2.1 copy-start.5
  620.7 1.1 copy-start.34
  621.2 3.0 copy-start.17
  621.2 3.1 copy-start.18
  621.2 3.1 copy-start.29
  627.1 3.6 copy-start.6
  633.3 1.6 copy-start.3
  636.4 251.8 %reduce-scatter.22.cloned.1.call-start = ((), (), s32[]{:S(2)}) async-start(), calls=%async_computation.18 | async-start | bytes 7864320 | tf_op jit(solution)/shard_map/reduce_scatter | solution.py:271
  752.6 16.8 %copy-start.31 = (bf16[768,768]{1,0:T(8,128)(2,1)S(1)}, bf16[768,768]{1,0:T(8,128)(2,1)}, u32[]{:S(2)}) copy-start(bf16[768,768]{1,0:T(8,128)(2,1)} %param.40) | copy-start | bytes 3538948
  779.2 235.8 %all-gather.11.cloned.1.call-start = ((), (), s32[]{:S(2)}) async-start(), calls=%async_computation.19 | async-start | bytes 7864320 | tf_op jit(solution)/shard_map/all_gather | solution.py:277
  888.1 4.0 copy-start.4
  888.1 4.2 copy-start.12
  895.6 1.7 copy-start.7
  898.8 261.4 %reduce-scatter.34.cloned.1.call-start = ((), (), s32[]{:S(2)}) async-start(), calls=%async_computation.25 | async-start | bytes 1769472
  909.4 253.0 %reduce-scatter.32.cloned.1.call-start = ((), (), s32[]{:S(2)}) async-start(), calls=%async_computation.24 | async-start | bytes 589824
  1108.0 56.0 %reduce-scatter.28.cloned.1.call-start = ((), (), s32[]{:S(2)}) async-start(), calls=%async_computation.22 | async-start | bytes 1474560
  1122.4 10.4 copy-start.33
  1122.4 44.9 %reduce-scatter.26.cloned.1.call-start = ((), (), s32[]{:S(2)}) async-start(), calls=%async_computation.21 | async-start | bytes 1769472 | tf_op jit(solution)/shard_map/reduce_scatter | solution.py:319
  1132.7 146.5 %reduce-scatter.24.cloned.1.call-start = ((), (), s32[]{:S(2)}) async-start(), calls=%async_computation.20 | async-start | bytes 7864320 | tf_op jit(solution)/shard_map/reduce_scatter | solution.py:295
  1132.8 10.4 copy-start.8
  1155.5 3.4 copy-start.37
  1155.5 194.2 %reduce-scatter.30.cloned.1.call-start = ((), (), s32[]{:S(2)}) async-start(), calls=%async_computation.23 | async-start | bytes 73728
  1158.9 200.2 %all-reduce.10.cloned.1.call-start = ((), (), s32[]{:S(2)}) async-start(), calls=%async_computation.27 | async-start | bytes 3538944 | tf_op jit(solution)/shard_map/psum | solution.py:330
  1286.1 79.0 %all-to-all-start.3 = ((bf16[2,4,128,768]{3,1,2,0:T(4,128)(2,1)}), bf16[2,4,128,768]{3,1,2,0:T(4,128)(2,1)S(1)}, u32[]{:S(2)}, u32[]{:S(2)}) async-start(bf16[2,4,128,768]{3,1,2,0:T(4,128)(2,1)} %copy.149), calls=%async_computation.7 | async-start | bytes 3145728 | tf_op jit(solution)/shard_map/all_to_all | solution.py:302
  1289.8 187.1 %all-reduce.8.cloned.1.call-start = ((), (), s32[]{:S(2)}) async-start(), calls=%async_computation.26 | async-start | bytes 917504 | tf_op jit(solution)/shard_map/psum | solution.py:337
  1359.0 4.4 copy-start.13
  1359.0 5.4 copy-start.15
  1365.1 4.6 copy-start.20
  1365.1 4.6 copy-start.26
  1366.8 113.3 %copy-start.1 = (bf16[7,128,768]{2,1,0:T(8,128)(2,1)S(1)}, bf16[7,128,768]{2,1,0:T(8,128)(2,1)}, u32[]{:S(2)}) copy-start(bf16[7,128,768]{2,1,0:T(8,128)(2,1)} %param.27) | copy-start | bytes 4128772
Sparse Core Ops, SparseCore 0:
  51.5 116.6 all-gather.4
  228.2 108.8 reduce-scatter.17
  342.0 116.0 all-gather.6
  508.8 108.8 reduce-scatter.19
  636.5 116.0 all-gather.8
  779.3 108.8 reduce-scatter.21
  898.9 116.0 all-gather.10
  1017.8 19.7 reduce-scatter.33
  1108.1 11.0 reduce-scatter.31
  1122.5 18.9 reduce-scatter.27
  1144.4 21.7 reduce-scatter.25
  1168.4 110.7 reduce-scatter.23
  1281.4 9.8 reduce-scatter.29
  1294.9 47.6 all-reduce.9
  1349.2 127.6 all-reduce.7
where the time goes:
time: 1490 us
  waiting for transfers between devices  1010 us (68%)
  matrix products  220 us (15%)
  other arithmetic  104 us (7%)
  local copies, waits for them, and re-layouts  62.7 us (4%)
  blocking collectives  62.1 us (4%)
  starting transfers between devices  16.5 us (1%)
  between operations  15.5 us (1%)
    all_gather x1, waiting for transfers between devices, on_device(): hidden_all = lax.all_gather(hidden_low, 'mp', axis=0, tiled=True)  116 us
    all_gather x1, waiting for transfers between devices, on_device(): ffn_all = lax.all_gather(ffn_low, 'mp', axis=0, tiled=True)  116 us
    reduce_scatter x1, waiting for transfers between devices, on_device(): lax.psum_scatter(grad_input.astype(jnp.bfloat16), 'mp', scatter_dimension...  111 us
    all_gather x1, waiting for transfers between devices, on_device(): rows_full = lax.all_gather(rows_part, 'mp', axis=1, tiled=True)  110 us
    reduce_scatter x1, waiting for transfers between devices, on_device(): lax.psum_scatter(up_part.astype(jnp.bfloat16), 'mp', scatter_dimension=0,...  109 us
    reduce_scatter x1, waiting for transfers between devices, on_device(): lax.psum_scatter(down_part.astype(jnp.bfloat16), 'mp', scatter_dimension=...  108 us
    all_gather x1, waiting for transfers between devices, on_device(): attn_all = lax.all_gather(attn_low, 'mp', axis=0, tiled=True)  105 us
    psum x1, waiting for transfers between devices, on_device(): lax.psum((g_bout, jnp.stack([g_gain_one, g_gain_two]), jnp.stack([g_shift...  105 us
  transfers between devices with their start and end apart: 19, of which 11 were waited for; matrix products, arithmetic and copies ran while one was open for 14% of the time, Pallas kernels for 0%

commit v1 on v0

v1 whole, which is shorter than its diff:
```python
import functools

import jax
import jax.numpy as jnp
from jax import lax
from jax.experimental import pallas as pl
from jax.experimental.pallas import tpu as pltpu
from jax.sharding import PartitionSpec as P

HEAD_DIM = 64
EPS = 1e-12
NEG = -1000000000.0
PRECISE = lax.Precision.HIGHEST
F32 = jnp.float32
BF16 = jnp.bfloat16
BLOCK = 512
VMEM_MOST = 62 * 1024 * 1024
NN = (((1,), (0,)), ((), ()))
NT = (((1,), (1,)), ((), ()))
TN = (((0,), (0,)), ((), ()))


def mm(left, right, dims=NN):
    return lax.dot_general(left, right, dims, preferred_element_type=F32)


def mm_exact(left, right, dims=NN):
    return lax.dot_general(left, right, dims, precision=PRECISE, preferred_element_type=F32)


def norm_parts(resid):
    center = resid - jnp.mean(resid, axis=-1, keepdims=True)
    spread = jnp.mean(center * center, axis=-1, keepdims=True)
    rstd = lax.rsqrt(spread + EPS)
    return center * rstd, rstd


def norm_back(upstream, xhat, rstd, gain):
    scaled = upstream * gain
    mean_u = jnp.mean(scaled, axis=-1, keepdims=True)
    mean_ux = jnp.mean(scaled * xhat, axis=-1, keepdims=True)
    return (scaled - mean_u - xhat * mean_ux) * rstd


def column_sum(value):
    return jnp.sum(value, axis=0, keepdims=True)


def mesh_place():
    g, b, z = lax.axis_index("grp"), lax.axis_index("batch"), lax.axis_index("mp")
    hi, lo, bit = g // 2, g % 2, b % 2
    return dict(
        g=g, b=b, z=z, hi=hi, lo=lo, bit=bit,
        far={"grp": (1 - hi) * 2 + lo}, twin={"grp": hi * 2 + 1 - lo}, side={"batch": b + 1 - 2 * bit},
        far_twin={"grp": (1 - hi) * 2 + 1 - lo},
    )


def remote(src, dst, send_sem, recv_sem, device):
    return pltpu.make_async_remote_copy(
        src_ref=src, dst_ref=dst, send_sem=send_sem, recv_sem=recv_sem,
        device_id=device, device_id_type=pl.DeviceIdType.MESH,
    )


def greet(at, batch_size, model_size):
    barrier = pltpu.get_barrier_semaphore()
    peers = [at["far"], at["twin"]]
    if batch_size > 1:
        peers += [{"batch": (at["b"] + j) % batch_size} for j in range(1, batch_size)]
    else:
        peers += [at["side"]]
    peers += [{"mp": (at["z"] + i) % model_size} for i in range(1, model_size)]
    for peer in peers:
        pl.semaphore_signal(barrier, inc=1, device_id=peer, device_id_type=pl.DeviceIdType.MESH)
    pl.semaphore_wait(barrier, len(peers))


def begin(copies):
    for copy in copies:
        copy.start()


def arrive(copies):
    for copy in copies:
        copy.wait_recv()


def sent(copies):
    for copy in copies:
        copy.wait_send()


SPLIT = 4


class Gather:
    def __init__(self, at, model_size, home, spot, send_sem, recv_sem, early=None):
        self.at, self.home, self.spot, self.early = at, home, spot, early
        self.send_sem, self.recv_sem = send_sem, recv_sem
        z, lo, hi, bit = at["z"], at["lo"], at["hi"], at["bit"]
        self.near = z + 1 - 2 * (z % 2)
        self.cross = (z + 2) % model_size
        self.chunks = (self.near, self.cross, (self.near + 2) % model_size)
        piece = home.shape[0] // 16
        half = pl.multiple_of(lo * (8 * piece), 16)
        self.one_a = pl.ds(pl.multiple_of(half + bit * (2 * piece) + hi * piece, 16), piece)
        self.one_b = pl.ds(pl.multiple_of(half + 4 * piece + hi * (2 * piece) + bit * piece, 16), piece)
        self.two_a = pl.ds(pl.multiple_of(half + bit * (2 * piece), 16), 2 * piece)
        self.two_b = pl.ds(pl.multiple_of(half + 4 * piece + hi * (2 * piece), 16), 2 * piece)
        self.half, self.step = half, 8 * piece // SPLIT

    def copies(self, stage, i):
        at, home, spot = self.at, self.home, self.spot

        def one(slot, src, dst, device):
            return remote(src, dst, self.send_sem.at[slot], self.recv_sem.at[slot], device)

        def same(slot, m, rows, device):
            return one(slot, spot.at[m, rows], spot.at[m, rows], device)

        m = self.chunks[i]
        if stage == 0 and i < 2:
            return [
                one(2 * i, home.at[self.one_a], spot.at[at["z"], self.one_a], {"mp": m}),
                one(2 * i + 1, home.at[self.one_b], spot.at[at["z"], self.one_b], {"mp": m}),
            ]
        if stage == 0:
            return [
                same(4, self.cross, self.one_a, {"mp": self.near}),
                same(5, self.cross, self.one_b, {"mp": self.near}),
            ]
        if stage == 1 and self.early is not None:
            return [
                one(6 + 2 * i, self.early.at[i, 0], spot.at[m, self.one_a], at["far"]),
                one(7 + 2 * i, self.early.at[i, 1], spot.at[m, self.one_b], at["side"]),
            ]
        if stage == 1:
            return [same(6 + 2 * i, m, self.one_a, at["far"]), same(7 + 2 * i, m, self.one_b, at["side"])]
        if stage == 2:
            return [same(12 + 2 * i, m, self.two_a, at["side"]), same(13 + 2 * i, m, self.two_b, at["far"])]
        return [
            same(18 + SPLIT * i + n, m, pl.ds(pl.multiple_of(self.half + n * self.step, 16), self.step), at["twin"])
            for n in range(SPLIT)
        ]

    def start(self):
        begin(self.copies(0, 1) + self.copies(0, 0))

    def early_copies(self, stage):
        def one(slot, src, dst, device):
            return remote(src, dst, self.send_sem.at[slot], self.recv_sem.at[slot], device)

        if stage == 0:
            return [
                one(2 * i + p, self.home.at[rows], self.early.at[i, p], {"mp": self.chunks[i]})
                for i in (1, 0)
                for p, rows in enumerate((self.one_a, self.one_b))
            ]
        return [one(4 + p, self.early.at[1, p], self.early.at[2, p], {"mp": self.near}) for p in range(2)]

    def own_pieces(self, sem):
        return [
            pltpu.make_async_copy(self.early.at[i, p], self.spot.at[self.chunks[i], rows], sem.at[2 * i + p])
            for i in range(3)
            for p, rows in enumerate((self.one_a, self.one_b))
        ]

    def advance(self, stage, *parts):
        for i in parts:
            arrive(self.copies(stage - 1, i))
            if stage == 1 and i == 1:
                begin(self.copies(0, 2))
            begin(self.copies(stage, i))

    def done(self, *parts):
        for i in parts:
            arrive(self.copies(3, i))

    def sent(self):
        for stage in range(0 if self.early is None else 1, 4):
            for i in range(3):
                sent(self.copies(stage, i))


GATHER_SEMS = 18 + 3 * SPLIT
PARTS = 2


class Reduce:
    def __init__(self, at, model_size, full, base, got_half, got_a, got_b, got_a2, got_b2, last, got_z, out,
                 send_sem, recv_sem, far_first=0, direct=False):
        self.far_first, self.direct = far_first, direct
        self.at, self.full, self.base, self.got_half = at, full, base, got_half
        self.got_a, self.got_b, self.got_a2, self.got_b2 = got_a, got_b, got_a2, got_b2
        self.last, self.got_z, self.out = last, got_z, out
        self.send_sem, self.recv_sem = send_sem, recv_sem
        z = at["z"]
        self.near, self.cross = z + 1 - 2 * (z % 2), (z + 2) % model_size

    def copies(self, stage, i=0):
        at, base = self.at, self.base
        b, lo, hi = at["b"], at["lo"], at["hi"]

        def one(slot, src, dst, device):
            return remote(src, dst, self.send_sem.at[slot], self.recv_sem.at[slot], device)

        m = chunk_of(at, i)
        if stage == 0:
            return [
                one(25 + 4 * i + 2 * y + p, self.full.at[m, y, 1 - lo, p], self.got_half.at[m, y, p], at["twin"])
                for y in range(2)
                for p in range(PARTS)
            ]
        if stage == 1 and i < self.far_first:
            return [
                one(4 + 2 * i, base.at[m, :, 0, 1 - hi], self.got_a.at[m], at["far"]),
                one(5 + 2 * i, base.at[m, :, 1, 1 - hi], self.got_b.at[m], at["far"]),
            ]
        if stage == 2 and i < self.far_first:
            return [
                one(12 + 2 * i, base.at[m, 1 - b, 0, hi], self.got_a2.at[m], at["side"]),
                one(13 + 2 * i, base.at[m, 1 - b, 1, hi], self.got_b2.at[m], at["side"]),
            ]
        if stage == 1:
            return [
                one(4 + 2 * i, base.at[m, :, 0, 1 - hi], self.got_a.at[m], at["far"]),
                one(5 + 2 * i, base.at[m, 1 - b, 1], self.got_b.at[m], at["side"]),
            ]
        if stage == 2:
            return [
                one(12 + 2 * i, base.at[m, 1 - b, 0, hi], self.got_a2.at[m], at["side"]),
                one(13 + 2 * i, base.at[m, b, 1, 1 - hi], self.got_b2.at[m], at["far"]),
            ]
        if stage == 3:
            device = {"mp": self.cross if i == 2 else self.near}
            return [one(20 + i, self.last.at[m], self.got_z.at[i], device)] if i < 3 else []
        mine = self.out.at[lo, :, hi]
        if stage == 4 and self.direct:
            return [one(23 + 18 * n, mine, mine, at[peer]) for n, peer in enumerate(("far", "twin", "far_twin"))]
        if stage == 4:
            return [one(23, mine, mine, at["far"])]
        if self.direct:
            return []
        return [one(24, self.out.at[lo], self.out.at[lo], at["twin"])]

    def start(self, i):
        begin(self.copies(0, i))

    def after_core(self, i, go_on=True):
        arrive(self.copies(0, i))
        m = chunk_of(self.at, i)

        def one(n, _):
            y, p, h = n // 4, n // 2 % 2, n % 2
            self.base[m, y, p, h] = self.base[m, y, p, h] + self.got_half[m, y, p, h]
            return 0

        lax.fori_loop(0, 8, one, 0)
        if go_on:
            begin(self.copies(1, i))

    def after_one(self, i):
        arrive(self.copies(1, i))
        m, b, hi, base = chunk_of(self.at, i), self.at["b"], self.at["hi"], self.base
        for h in range(2):
            base[m, h, 0, hi] = base[m, h, 0, hi] + self.got_a[m, h]
            if i < self.far_first:
                base[m, h, 1, hi] = base[m, h, 1, hi] + self.got_b[m, h]
            else:
                base[m, b, 1, h] = base[m, b, 1, h] + self.got_b[m, h]
        begin(self.copies(2, i))

    def after_two(self, i, go_on=True):
        arrive(self.copies(2, i))
        m, b, hi, base = chunk_of(self.at, i), self.at["b"], self.at["hi"], self.base
        found = [base[m, b, 0, hi] + self.got_a2[m], base[m, b, 1, hi] + self.got_b2[m]]
        if i == 2:
            arrive(self.copies(3, 0))
        for p in range(PARTS):
            self.last[m, p] = found[p] + self.got_z[0, p] if i == 2 else found[p]
        if go_on:
            begin(self.copies(3, i))

    def total(self, p):
        z = self.at["z"]
        found = self.last[z, p].astype(F32) + self.got_z[1, p].astype(F32) + self.got_z[2, p].astype(F32)
        return found.astype(BF16)

    def after_three(self):
        arrive(self.copies(3, 1) + self.copies(3, 2))
        for p in range(PARTS):
            self.out[self.at["lo"], p, self.at["hi"]] = self.total(p)
        begin(self.copies(4))

    def hand_over(self, own_ref, hand_ref):
        arrive(self.copies(3, 1))
        own_ref[...] = self.base[self.at["z"]]
        hand_ref[0] = self.last[self.cross]
        hand_ref[1] = self.got_z[1]

    def after_four(self):
        arrive(self.copies(4))
        begin(self.copies(5))

    def done(self):
        arrive(self.copies(4) if self.direct else self.copies(5))

    def sent(self):
        for stage in range(6):
            for i in range(4 if stage < 4 else 1):
                sent(self.copies(stage, i))

    def sent_early(self):
        for stage, count in enumerate((4, 3, 3, 2)):
            for i in range(count):
                sent(self.copies(stage, i))


class Finish:
    def __init__(self, at, model_size, own, hand, got_a, got_b, got_a2, got_b2, got_z, out, send_sem, recv_sem):
        self.at, self.own, self.hand, self.out = at, own, hand, out
        self.got_a, self.got_b, self.got_a2, self.got_b2, self.got_z = got_a, got_b, got_a2, got_b2, got_z
        self.send_sem, self.recv_sem = send_sem, recv_sem
        self.cross = (at["z"] + 2) % model_size

    def copies(self, stage):
        at, own = self.at, self.own
        b, lo, hi = at["b"], at["lo"], at["hi"]

        def one(slot, src, dst, device):
            return remote(src, dst, self.send_sem.at[slot], self.recv_sem.at[slot], device)

        if stage == 0:
            return [one(0, self.hand.at[0], self.got_z, {"mp": self.cross})]
        if stage == 1:
            return [
                one(1, own.at[:, 0, 1 - hi], self.got_a, at["far"]),
                one(2, own.at[1 - b, 1], self.got_b, at["side"]),
            ]
        if stage == 2:
            return [
                one(3, self.got_a.at[1 - b], self.got_a2, at["side"]),
                one(4, self.got_b.at[1 - hi], self.got_b2, at["far"]),
            ]
        if stage == 3:
            return [one(5, self.out.at[lo, :, hi], self.out.at[lo, :, hi], at["far"])]
        return [one(6, self.out.at[lo], self.out.at[lo], at["twin"])]

    def start(self):
        begin(self.copies(1) + self.copies(0))

    def after_one(self):
        arrive(self.copies(1))
        b, hi = self.at["b"], self.at["hi"]
        for h in range(2):
            self.got_a[h] = self.got_a[h] + self.own[h, 0, hi]
            self.got_b[h] = self.got_b[h] + self.own[b, 1, h]
        begin(self.copies(2))

    def after_two(self):
        arrive(self.copies(2) + self.copies(0))
        b, lo, hi = self.at["b"], self.at["lo"], self.at["hi"]
        halves = ((self.got_a[b], self.got_a2[...]), (self.got_b[hi], self.got_b2[...]))
        for p, (held, got) in enumerate(halves):
            total = held.astype(F32) + got.astype(F32) + self.hand[1, p].astype(F32) + self.got_z[p].astype(F32)
            self.out[lo, p, hi] = total.astype(BF16)
        begin(self.copies(3))

    def after_three(self):
        arrive(self.copies(3))
        begin(self.copies(4))

    def done(self):
        arrive(self.copies(4))

    def sent(self):
        for stage in range(5):
            sent(self.copies(stage))


REDUCE_SEMS = 60


def chunk_of(at, i):
    high, low = at["z"] // 2, at["z"] % 2
    flip_high, flip_low = 1 - i % 2, 1 - i // 2
    return 2 * (high + flip_high - 2 * high * flip_high) + low + flip_low - 2 * low * flip_low


def reduce_scratch(model_size, piece, dim):
    low = lambda *shape: pltpu.VMEM(shape, BF16)
    return [
        low(model_size, 2, PARTS, 2, piece, dim),
        low(model_size, 2, piece, dim),
        low(model_size, 2, piece, dim),
        low(model_size, piece, dim),
        low(model_size, piece, dim),
        low(model_size, PARTS, piece, dim),
        low(3, PARTS, piece, dim),
    ]


def pack_places(dim, width):
    ends = [dim]
    for size in (width, 16, 8, 8 * dim // width, 8 * dim // width):
        ends.append(ends[-1] + size)
    return [slice(first, last) for first, last in zip(ends[:-1], ends[1:])]


def pack_rows(dim, width):
    return -(-pack_places(dim, width)[-1].stop // 128) * 128


def student_step(
    stud_ref, own_ref, query_ref, w2_ref, bmid, w3_ref, b3_ref,
    dstud_ref, gw2_ref, gw3_ref, gsmall_ref, classes, pairs,
):
    row_count, seq, width = stud_ref.shape
    head = own_ref.shape[1] - seq
    tag_cells = [
        [own_ref[r : r + 1, p : p + 1] for p in range(2 * pairs)] for r in range(row_count)
    ]
    labels = jnp.concatenate([cells[p] for cells in tag_cells for p in range(pairs)], axis=0)
    weights = jnp.concatenate([cells[pairs + p] for cells in tag_cells for p in range(pairs)], axis=0)
    half = width // 2
    lane = lax.broadcasted_iota(jnp.int32, (2 * pairs, width), 1)
    row = lax.broadcasted_iota(jnp.int32, (2 * pairs, width), 0)
    mine = (lane >= half) == (row >= pairs)
    query_rows = jnp.where(mine, query_ref[...].reshape(1, width) * half ** (-0.5), 0.0)
    pair_of = lax.rem(lax.broadcasted_iota(jnp.int32, (2 * pairs, seq), 0), pairs).astype(F32)
    members, shares_all, pooled_all = [], [], []
    for r in range(row_count):
        scores = mm_exact(query_rows, stud_ref[r], NT)
        member = own_ref[r : r + 1, head:] == pair_of
        masked = jnp.where(member, scores, NEG)
        terms = jnp.exp(masked - jnp.max(masked, axis=1, keepdims=True))
        shares = terms / jnp.sum(terms, axis=1, keepdims=True)
        pooled = jnp.where(mine, mm_exact(shares, stud_ref[r]), 0.0)
        members.append(member)
        shares_all.append(shares)
        pooled_all.append(pooled[:pairs] + pooled[pairs:])
    pooled = jnp.concatenate(pooled_all, axis=0)
    middle = jnp.tanh(mm_exact(pooled, w2_ref[...]) + bmid)
    logits = mm_exact(middle, w3_ref[...], NT) + b3_ref[...]
    class_of = lax.broadcasted_iota(jnp.int32, logits.shape, 1)
    logits = jnp.where(class_of < classes, logits, NEG)
    terms = jnp.exp(logits - jnp.max(logits, axis=1, keepdims=True))
    chance = terms / jnp.sum(terms, axis=1, keepdims=True)
    grad_logits = weights * (chance - jnp.where(class_of.astype(F32) == labels, 1.0, 0.0))
    gw3_ref[...] = mm_exact(grad_logits, middle, TN)[: gw3_ref.shape[0]]
    grad_pre = mm_exact(grad_logits, w3_ref[...]) * (1.0 - middle * middle)
    gw2_ref[...] = mm_exact(pooled, grad_pre, TN)
    grad_pooled = mm_exact(grad_pre, w2_ref[...], NT)
    grad_query = jnp.zeros((1, width), F32)
    grad_bias = jnp.zeros((1, width), F32)
    for r in range(row_count):
        part = grad_pooled[r * pairs : (r + 1) * pairs]
        grad_parts = jnp.where(mine, jnp.concatenate([part, part], axis=0), 0.0)
        shares = shares_all[r]
        grad_shares = mm_exact(grad_parts, stud_ref[r], NT)
        inner = jnp.sum(shares * grad_shares, axis=1, keepdims=True)
        grad_scores = jnp.where(members[r], shares * (grad_shares - inner), 0.0)
        grad_hidden = mm_exact(
            jnp.concatenate([shares, grad_scores], axis=0),
            jnp.concatenate([grad_parts, query_rows], axis=0),
            TN,
        )
        low = grad_hidden.astype(BF16)
        dstud_ref[r] = low
        grad_bias += column_sum(low.astype(F32))
        found = mm_exact(grad_scores, stud_ref[r]) * half ** (-0.5)
        grad_query += column_sum(jnp.where(mine, found, 0.0))
    gsmall_ref[0:1] = grad_bias
    gsmall_ref[1:2] = column_sum(grad_pre)
    gsmall_ref[2:3] = grad_query
    gsmall_ref[3:4] = column_sum(grad_logits)
    gsmall_ref[4:8] = jnp.zeros((4, width), F32)


def gelu_parts(value):
    size = jnp.abs(value)
    bell = jnp.exp(value * value * -0.5)
    base = 1.0 + (0.3275911 * 0.5 ** 0.5) * size
    t = pl.reciprocal(base, approx=True)
    t = t * (2.0 - base * t)
    terms = ((((1.061405429 * t - 1.453152027) * t + 1.421413741) * t - 0.284496736) * t + 0.254829592) * t
    tail = 0.5 * terms * bell
    return jnp.where(value < 0.0, tail, 1.0 - tail), bell * 0.3989422804014327


COLUMNS = 256


def ffn_kernel(
    classes, pairs, scatter,
    xhat1_ref, rstd1_ref, gain_ref, shift_ref, wb_ref, wc_home, early_ref, vecs_ref, bdown_ref, cot_ref, own_ref,
    sw1_ref, sbias_ref, query_ref, w2_in, w3_in, b3_in,
    mixed_ref, gres_ref, dwb_ref, out_ref, hand_ref, pack_ref,
    w2_ref, w3_ref, b3_ref, gbup_ref, gvec_ref, gsw1_ref, act_ref, slope_ref, xhat2_ref, rstd2_ref,
    stud_ref, dstud_ref, low_ref, flip_ref, wc_ref, dwc_ref, wsend, wrecv, msend, mrecv, local_sem, piece_sem, *parts,
):
    row_count, seq, dim = xhat1_ref.shape
    model_size = wb_ref.shape[0]
    inner = wb_ref.shape[2]
    per_row = seq // BLOCK
    blocks = row_count * per_row
    width = sw1_ref.shape[1]
    at = mesh_place()
    gather = Gather(at, model_size, wc_home, wc_ref, wsend, wrecv, early_ref)
    own_pieces = gather.own_pieces(piece_sem)
    own_copy = pltpu.make_async_copy(wc_home, wc_ref.at[at["z"]], local_sem.at[0])
    own_copy.start()
    for copy in own_pieces:
        copy.start()
    greet(at, 2 if scatter else 1, model_size)
    for i in (1, 0, 2):
        begin(gather.copies(1, i))
    if scatter:
        reducer = Reduce(at, model_size, dwc_ref, dwc_ref.at[:, :, at["lo"]], *parts, None, msend, mrecv)

    w2_at, w3_at, small_at, vec_at, bup_at = pack_places(dim, width)
    sb1, bmid = sbias_ref[0:1], sbias_ref[1:2]
    w2_ref[...] = w2_in[...].astype(F32)
    w3_ref[...] = jnp.zeros_like(w3_ref)
    w3_ref[:classes] = w3_in[...].astype(F32)
    b3_ref[...] = jnp.zeros_like(b3_ref)
    b3_ref[:, :classes] = b3_in[...].reshape(1, classes)
    gain_one, gain_two = gain_ref[0:1], gain_ref[1:2]
    shift_one, shift_two = shift_ref[0:1], shift_ref[1:2]

    def live(r):
        cells = [own_ref[i : i + 1, 2 * pairs : 2 * pairs + 1] for i in range(row_count)]
        return sum(jnp.where(r == i, 1.0, 0.0) * cells[i] for i in range(row_count))

    def place(t):
        return t // per_row, pl.ds(pl.multiple_of(t % per_row * BLOCK, BLOCK), BLOCK)

    def prepare(t, _):
        r, part = place(t)
        hidden = xhat1_ref[r, part] * gain_one + shift_one
        low_ref[t] = hidden.astype(BF16)
        xhat2_ref[r, part] = hidden + bdown_ref[...].reshape(1, dim)
        return 0

    lax.fori_loop(0, blocks, prepare, 0)
    for copy in own_pieces:
        copy.wait()
    def during(m, table):
        for when, actions in table.items():
            @pl.when(m == when)
            def _():
                for action, *args in actions:
                    action(*args)

    def up(m, _):
        during(m, {
            1: [(gather.advance, 2, 1, 0)],
            2: [(gather.advance, 2, 2), (gather.advance, 3, 1)],
            3: [(gather.advance, 3, 0)],
        })

        def one(t, _):
            low = low_ref[t]
            for c in range(0, inner, COLUMNS):
                columns = slice(c, c + COLUMNS)
                pre = mm(low, wb_ref[m, :, columns]) + vecs_ref[m, 1:2, columns]
                cdf, pdf = gelu_parts(pre)
                act_ref[m, t, :, columns] = (pre * cdf).astype(BF16)
                slope_ref[m, t, :, columns] = (cdf + pre * pdf).astype(BF16)
            return 0

        lax.fori_loop(0, blocks, one, 0)
        return 0

    lax.fori_loop(0, model_size, up, 0)
    gather.advance(3, 2)
    own_copy.wait()

    def down(m):
        def one(t, _):
            r, part = place(t)
            xhat2_ref[r, part] = xhat2_ref[r, part] + mm(act_ref[m, t], wc_ref[m])
            return 0

        lax.fori_loop(0, blocks, one, 0)

    down(at["z"])
    for i in (1, 0, 2):
        gather.done(i)
        down(gather.chunks[i])

    def norm_two(t, _):
        r, part = place(t)
        xhat, rstd = norm_parts(xhat2_ref[r, part])
        xhat2_ref[r, part] = xhat
        rstd2_ref[r, part] = rstd
        hidden_two = xhat * gain_two + shift_two
        mixed_ref[r, part] = (hidden_two * live(r)).astype(BF16)
        stud_ref[r, part] = mm(hidden_two.astype(BF16), sw1_ref[...]) + sb1
        return 0

    lax.fori_loop(0, blocks, norm_two, 0)
    student_step(
        stud_ref, own_ref, query_ref, w2_ref, bmid, w3_ref, b3_ref,
        dstud_ref, pack_ref.at[w2_at], pack_ref.at[w3_at], pack_ref.at[small_at], classes, pairs,
    )
    gvec_ref[...] = jnp.zeros_like(gvec_ref)
    gsw1_ref[...] = jnp.zeros_like(gsw1_ref)
    gbup_ref[...] = jnp.zeros_like(gbup_ref)

    def norm_two_back(t, _):
        r, part = place(t)
        xhat = xhat2_ref[r, part]
        two_low = (xhat * gain_two + shift_two).astype(BF16)
        grad_low = dstud_ref[r, part]
        gsw1_ref[...] += mm(grad_low, two_low, TN)
        upstream = cot_ref[r, part].astype(F32) * live(r) + mm(grad_low, sw1_ref[...], NT)
        gvec_ref[1:2] += column_sum(upstream * xhat)
        gvec_ref[3:4] += column_sum(upstream)
        grad = norm_back(upstream, xhat, rstd2_ref[r, part], gain_two)
        low = grad.astype(BF16)
        gvec_ref[4:5] += column_sum(low.astype(F32))
        gres_ref[r, part] = grad
        low_ref[t] = low
        flip_ref[:, pl.ds(pl.multiple_of(t * BLOCK, BLOCK), BLOCK)] = low.T
        return 0

    lax.fori_loop(0, blocks, norm_two_back, 0)
    half = dim // 2

    def weight_grads(out, right_ref, m):
        def one(y, _):
            part = pl.ds(pl.multiple_of(y * half, 128), half)
            total = mm(flip_ref[part, :], right_ref[m].reshape(blocks * BLOCK, inner)).astype(BF16)
            out[m, y] = total.reshape(out.shape[2:])
            return 0

        lax.fori_loop(0, 2, one, 0)

    def first_grads(i, _):
        weight_grads(dwc_ref, act_ref, chunk_of(at, i))
        if scatter:
            during(i, {n: [(reducer.start, n)] for n in range(model_size)})
        return 0

    lax.fori_loop(0, model_size, first_grads, 0)
    def backward(m, _):
        if scatter:
            during(m, {
                1: [(reducer.after_core, 0)],
                2: [(reducer.after_core, 1), (reducer.after_one, 0)],
                3: [(reducer.after_two, 0), (reducer.after_one, 1), (reducer.after_core, 2)],
            })

        def one(t, _):
            r, part = place(t)
            grad_pre = (mm(low_ref[t], wc_ref[m], NT) * slope_ref[m, t].astype(F32)).astype(BF16)
            slope_ref[m, t] = grad_pre
            gbup_ref[m] += column_sum(grad_pre.astype(F32))
            gres_ref[r, part] = gres_ref[r, part] + mm(grad_pre, wb_ref[m], NT)
            return 0

        lax.fori_loop(0, blocks, one, 0)
        return 0

    lax.fori_loop(0, model_size, backward, 0)

    def norm_one_back(t, _):
        r, part = place(t)
        upstream = gres_ref[r, part]
        xhat = xhat1_ref[r, part]
        gvec_ref[0:1] += column_sum(upstream * xhat)
        gvec_ref[2:3] += column_sum(upstream)
        resid = norm_back(upstream, xhat, rstd1_ref[r, part], gain_one)
        gres_ref[r, part] = resid
        gvec_ref[5:6] += column_sum(resid.astype(BF16).astype(F32))
        flip_ref[:, pl.ds(pl.multiple_of(t * BLOCK, BLOCK), BLOCK)] = (xhat * gain_one + shift_one).astype(BF16).T
        return 0

    lax.fori_loop(0, blocks, norm_one_back, 0)
    def second_grads(m, _):
        if scatter:
            during(m, {
                1: [(reducer.after_two, 1), (reducer.after_one, 2)],
                3: [(reducer.after_core, 3, False), (reducer.after_two, 2, False)],
            })
        weight_grads(dwb_ref, slope_ref, m)
        return 0

    lax.fori_loop(0, model_size, second_grads, 0)
    for m in range(model_size):
        bup = gbup_ref[m]
        for j in range(dim // width):
            pack_ref[bup_at.start + j * 8 + m : bup_at.start + j * 8 + m + 1] = bup[:, j * width : (j + 1) * width]
    for j in range(dim // width):
        columns = slice(j * width, (j + 1) * width)
        pack_ref[columns] = gsw1_ref[:, columns]
        pack_ref[vec_at.start + j * 8 : vec_at.start + j * 8 + 8] = gvec_ref[:, columns]
        if model_size < 8:
            first = bup_at.start + j * 8
            pack_ref[first + model_size : first + 8] = jnp.zeros((8 - model_size, width), F32)
    pack_ref[bup_at.stop :] = jnp.zeros((pack_ref.shape[0] - bup_at.stop, width), F32)
    if scatter:
        reducer.hand_over(out_ref, hand_ref)
        reducer.sent_early()
    else:
        out_ref[...] = dwc_ref[...]
        hand_ref[...] = jnp.zeros_like(hand_ref)
    gather.sent()


def ffn_both(xhat1, rstd1, gain, shift, w_b, w_c, early, vecs, b_down, cot, own, pairs, scatter,
             s_w1, s_bias, s_query, s_w2, s_w3, s_b3):
    rows, seq, dim = xhat1.shape
    model_size = w_b.shape[0]
    inner = w_b.shape[2]
    width = s_w1.shape[1]
    classes = s_w3.shape[1]
    blocks = rows * seq // BLOCK
    piece = dim // 16
    grid_shape = (model_size, 2, 2, PARTS, 2, piece, inner)
    low = lambda *shape: pltpu.VMEM(shape, BF16)
    f32 = lambda *shape: pltpu.VMEM(shape, F32)
    dma = pltpu.SemaphoreType.DMA
    vmem = pl.BlockSpec(memory_space=pltpu.VMEM)
    hbm = pl.BlockSpec(memory_space=pl.ANY)
    return pl.pallas_call(
        functools.partial(ffn_kernel, classes, pairs, scatter),
        in_specs=[vmem] * 5 + [hbm, hbm] + [vmem] * 10,
        out_specs=[vmem] * 6,
        out_shape=(
            jax.ShapeDtypeStruct((rows, seq, dim), BF16),
            jax.ShapeDtypeStruct((rows, seq, dim), F32),
            jax.ShapeDtypeStruct(grid_shape, BF16),
            jax.ShapeDtypeStruct(grid_shape[1:2] + grid_shape[3:] if scatter else grid_shape, BF16),
            jax.ShapeDtypeStruct((2, PARTS, piece, inner), BF16),
            jax.ShapeDtypeStruct((pack_rows(dim, width), width), F32),
        ),
        scratch_shapes=[
            f32(width, width),
            f32(width, width),
            f32(1, width),
            f32(model_size, 1, inner),
            f32(8, dim),
            f32(width, dim),
            low(model_size, blocks, BLOCK, inner),
            low(model_size, blocks, BLOCK, inner),
            f32(rows, seq, dim),
            f32(rows, seq, 1),
            f32(rows, seq, width),
            low(rows, seq, width),
            low(blocks, BLOCK, dim),
            low(dim, rows * seq),
            low(model_size, inner, dim),
            low(*grid_shape),
            dma((GATHER_SEMS,)),
            dma((GATHER_SEMS,)),
            dma((REDUCE_SEMS,)),
            dma((REDUCE_SEMS,)),
            dma((1,)),
            dma((6,)),
            *(reduce_scratch(model_size, piece, inner) if scatter else ()),
        ],
        compiler_params=pltpu.CompilerParams(
            vmem_limit_bytes=VMEM_MOST, collective_id=1, has_side_effects=True
        ),
        name="ffn_both",
    )(
        xhat1, rstd1, gain, shift, w_b, w_c, early, vecs, b_down, cot, own,
        s_w1, s_bias, s_query, s_w2, s_w3.T, s_b3,
    )


TILE_Q = 256
TILE_BACK = 64


def backward_group(grad_ctx, ctx_of, load, store, mask, lse_of, group_dim, p_ref, s_ref):
    scale = HEAD_DIM ** (-0.5)
    for j in range(group_dim // HEAD_DIM):
        rows = slice(j * HEAD_DIM, (j + 1) * HEAD_DIM)
        k_rows = slice(group_dim + rows.start, group_dim + rows.stop)
        v_rows = slice(2 * group_dim + rows.start, 2 * group_dim + rows.stop)
        q_t = load(rows) * scale
        k_t = load(k_rows)
        v_t = load(v_rows)
        d_t = grad_ctx[rows]
        seq = q_t.shape[1]
        inner = column_sum(d_t.astype(F32) * ctx_of(rows).astype(F32))
        lse = lse_of(j)
        k_n, v_n = k_t.T, v_t.T
        probs_ref, grads_ref = p_ref.at[j % 2], s_ref.at[j % 2]
        for q0 in range(0, seq, TILE_Q):
            columns = slice(q0, q0 + TILE_Q)
            q, d = q_t[:, columns], d_t[:, columns]
            for k0 in range(0, seq, TILE_BACK):
                part = slice(k0, k0 + TILE_BACK)
                probs = jnp.exp(mm(k_n[part], q) + mask[part, columns] - lse[:, columns])
                grad_probs = mm(v_n[part], d)
                probs_ref[part, columns] = probs.astype(BF16)
                grads_ref[part, columns] = (probs * (grad_probs - inner[:, columns])).astype(BF16)
        store(rows, mm(k_t * scale, grads_ref[...]).astype(BF16))
        store(k_rows, mm(q_t, grads_ref[...], NT).astype(BF16))
        store(v_rows, mm(d_t, probs_ref[...], NT).astype(BF16))


def attn_backward_kernel(
    x_ref, gres_ref, wa_ref, qkv_ref, ctx_ref, lse_ref, own_ref, dx_ref, dwa_ref, bias_ref,
    mask_ref, acc_ref, work_ref, xflip_ref, gflip_ref, p_ref, s_ref,
):
    row_count, seq, dim = x_ref.shape
    model_size = wa_ref.shape[0]
    group_dim = ctx_ref.shape[2]
    bias_ref[...] = jnp.zeros_like(bias_ref)
    seg_rows = own_ref[:, own_ref.shape[1] - seq :]
    seg_cols = seg_rows.T
    for r in range(row_count):
        mask_ref[...] = jnp.where(seg_cols[:, r : r + 1] == seg_rows[r : r + 1], 0.0, NEG)
        acc_ref[...] = gres_ref[r]
        grad_low = gres_ref[r].astype(BF16)
        columns = slice(r * seq, (r + 1) * seq)
        gflip_ref[:, columns] = grad_low.T
        xflip_ref[:, columns] = x_ref[r].T

        def one_group(m, _):
            grad_ctx = mm(wa_ref[m, 3 * group_dim :, :], grad_low, NT).astype(BF16)

            def store(rows, value):
                work_ref[r, m, rows, :] = value

            backward_group(
                grad_ctx, lambda rows: ctx_ref[r, m, rows, :], lambda rows: qkv_ref[r, m, rows, :], store,
                mask_ref, lambda j: lse_ref[r, m, j : j + 1, :], group_dim, p_ref, s_ref,
            )
            grads = work_ref[r, m]
            bias_ref[m] += mm(jnp.ones((8, seq), BF16), grads, NT)
            acc_ref[...] += mm(grads, wa_ref[m, : 3 * group_dim, :], TN)
            return 0

        lax.fori_loop(0, model_size, one_group, 0)
        dx_ref[r] = acc_ref[...].astype(BF16)

    def weight_grads(i, _):
        m, part = i // 2, pl.ds(pl.multiple_of(i % 2 * (dim // 2), 128), dim // 2)
        left, right = 0.0, 0.0
        for r in range(row_count):
            columns = slice(r * seq, (r + 1) * seq)
            left += mm(xflip_ref[part, columns], work_ref[r, m], NT)
            right += mm(gflip_ref[part, columns], ctx_ref[r, m], NT)
        dwa_ref[m, part, : 3 * group_dim] = left.astype(BF16)
        dwa_ref[m, part, 3 * group_dim :] = right.astype(BF16)
        return 0

    lax.fori_loop(0, 2 * model_size, weight_grads, 0)


def attn_backward(x, gres, w_a, qkv, ctx, lse, own):
    rows, seq, dim = x.shape
    model_size = w_a.shape[0]
    group_dim = dim // model_size
    return pl.pallas_call(
        attn_backward_kernel,
        out_shape=(
            jax.ShapeDtypeStruct((rows, seq, dim), BF16),
            jax.ShapeDtypeStruct((model_size, dim, 4 * group_dim), BF16),
            jax.ShapeDtypeStruct((model_size, 8, 3 * group_dim), F32),
        ),
        scratch_shapes=[
            pltpu.VMEM((seq, seq), F32),
            pltpu.VMEM((seq, dim), F32),
            pltpu.VMEM((rows, model_size, 3 * group_dim, seq), BF16),
            pltpu.VMEM((dim, rows * seq), BF16),
            pltpu.VMEM((dim, rows * seq), BF16),
            pltpu.VMEM((2, seq, seq), BF16),
            pltpu.VMEM((2, seq, seq), BF16),
        ],
        compiler_params=pltpu.CompilerParams(vmem_limit_bytes=VMEM_MOST),
        name="attn_backward",
    )(x, gres, w_a, qkv, ctx, lse, own)
def slot_of_rows(exit_ref, target_ref, depth):
    count = exit_ref.shape[0]
    flat = []
    for i in range(count):
        rank = 0
        for h in range(i):
            rank = rank + jnp.where(target_ref[h] == target_ref[i], 1 - exit_ref[h], 0)
        flat.append(jnp.where(exit_ref[i] == 0, target_ref[i] * depth + rank, -1))
    return flat


def pick_of_slots(tag_ref, depth, flag_at, capacity):
    seen = jnp.zeros((1, 1), F32)
    picks = []
    for k in range(tag_ref.shape[0] * depth):
        live = tag_ref[k // depth, k % depth : k % depth + 1, flag_at : flag_at + 1]
        picks.append([jnp.where(seen == float(c), live, 0.0) for c in range(min(capacity, k + 1))])
        seen = seen + live
    return picks


def slots_of_tags(tag_ref, depth, flag_at, capacity):
    seen, slots = 0, []
    for k in range(tag_ref.shape[0] * depth):
        cell = tag_ref[k // depth, k % depth : k % depth + 1, flag_at : flag_at + 1]
        live = jnp.where(jnp.sum(cell) > 0.5, 1, 0)
        slots.append((jnp.minimum(seen, capacity - 1), live))
        seen = seen + live
    return slots


TOKENS = 32
CUTS = 3


def enter_kernel(
    depth, pairs,
    exit_ref, target_ref, rows_ref, seg_ref, lab_ref, wt_ref, wqkv_ref, wout_ref, bqv_ref, bup_ref, bout_ref,
    wb_loc, wc_loc,
    own_ref, got_tags_ref, vecs_ref, x_out, wa_out, wb_ref, early_ref,
    qkv_ref, ctx_ref, lse_ref, xhat_ref, rstd_ref,
    tags_ref, vec_ref, wa_loc, slot_ref, part_ref, x_ref, wa_ref, tag_ref, taggot_ref, taglocal_ref, vecgot_ref,
    mask_ref, acc_ref, wsend, wrecv, rsend, rrecv, local_sem, *got_refs,
):
    row_count, token_part, dim = rows_ref.shape
    own_rows, seq = x_ref.shape[:2]
    model_size = wa_ref.shape[0]
    batch_size = taggot_ref.shape[0]
    capacity = own_rows * model_size
    group_dim = wout_ref.shape[0]
    flag_at = 2 * pairs
    head = tag_ref.shape[2] - seq
    at = mesh_place()
    b, z = at["b"], at["z"]
    gathers = [
        Gather(at, model_size, home, spot, wsend.at[k], wrecv.at[k])
        for k, (home, spot) in enumerate(((wa_loc, wa_ref), (wb_loc, wb_ref)))
    ]
    first_gather, second_gather = gathers
    third_gather = Gather(at, model_size, wc_loc, None, wsend.at[2], wrecv.at[2], early_ref)
    vec_first = (CUTS + 1) * batch_size + CUTS * model_size

    def vec_copies():
        return [
            remote(vec_ref, vecgot_ref.at[z], rsend.at[vec_first + i], rrecv.at[vec_first + i],
                   {"mp": (z + i) % model_size})
            for i in range(1, model_size)
        ]

    wide = dim // CUTS

    def batch_copies(cut):
        columns = pl.ds(cut * wide, wide)
        copies = []
        for j in range(1, batch_size):
            t = (b + j) % batch_size
            n = cut * batch_size + j
            copies.append(remote(slot_ref.at[pl.ds(t * depth, depth), :, columns],
                                 got_refs[cut].at[pl.ds(b * depth, depth)],
                                 rsend.at[n], rrecv.at[n], {"batch": t}))
            if cut == 0:
                n = CUTS * batch_size + j
                copies.append(remote(tag_ref.at[t], taggot_ref.at[b], rsend.at[n], rrecv.at[n], {"batch": t}))
        return copies

    mine = pl.ds(pl.multiple_of(z * token_part, 128), token_part)

    def row_copies(cut, r):
        columns = pl.ds(cut * wide, wide)
        first = (CUTS + 1) * (batch_size + model_size) + (cut * own_rows + r) * model_size
        return [
            remote(part_ref.at[(z + i) % model_size * own_rows + r, :, columns], x_ref.at[r, mine, columns],
                   rsend.at[first + i], rrecv.at[first + i], {"mp": (z + i) % model_size})
            for i in range(1, model_size)
        ]

    def local_copies():
        return [
            pltpu.make_async_copy(gather.home, gather.spot.at[z], local_sem.at[k])
            for k, gather in enumerate(gathers)
        ]

    for j in range(3):
        wa_loc[j * group_dim : (j + 1) * group_dim, :] = wqkv_ref[j]
    wa_loc[3 * group_dim :, :] = wout_ref[...]
    vec_ref[...] = jnp.zeros_like(vec_ref)
    vec_ref[0:1, :group_dim] = bqv_ref[0:1]
    vec_ref[0:1, 2 * group_dim : 3 * group_dim] = bqv_ref[1:2]
    vec_ref[1:2] = bup_ref[...].reshape(1, dim)
    greet(at, batch_size, model_size)
    first_gather.start()
    begin(vec_copies())
    begin(local_copies())

    flat = slot_of_rows(exit_ref, target_ref, depth)
    tags_ref[...] = jnp.zeros_like(tags_ref)
    taglocal_ref[0] = jnp.zeros_like(taglocal_ref[0])
    taglocal_ref[0, :pairs, :row_count] = lab_ref[...].astype(F32)
    taglocal_ref[0, pairs : 2 * pairs, :row_count] = wt_ref[...].astype(F32)
    tags_ref[:, : 2 * pairs] = taglocal_ref[0, : 2 * pairs, :128].T[: tags_ref.shape[0]]
    tags_ref[:row_count, flag_at : flag_at + 1] = jnp.ones((row_count, 1), F32)
    tags_ref[:row_count, head:] = seg_ref[...].astype(F32)
    tag_ref[...] = jnp.zeros_like(tag_ref)

    def taken(k):
        hits = [jnp.where(flat[r] == k, 1, 0) for r in range(row_count)]
        return sum(r * hits[r] for r in range(row_count)), sum(hits).astype(F32)

    def fill(t, dst_ref, cut):
        columns = pl.ds(cut * wide, wide)
        for s in range(depth):
            row, there = taken(t * depth + s)
            found = (rows_ref[row, :, columns].astype(F32) * there).astype(BF16)
            if dst_ref is None:
                got_refs[cut][t * depth + s] = found
            else:
                dst_ref[t * depth + s, :, columns] = found

    def fill_tags(t):
        for s in range(depth):
            total = jnp.zeros((1, tags_ref.shape[1]), F32)
            for r in range(row_count):
                total += jnp.where(flat[r] == t * depth + s, 1.0, 0.0) * tags_ref[r : r + 1]
            tag_ref[t, s : s + 1] = total

    for j in range(1, batch_size):
        fill_tags((b + j) % batch_size)
    for cut in range(CUTS):
        for j in range(1, batch_size):
            fill((b + j) % batch_size, slot_ref, cut)
        if cut == 0:
            begin(batch_copies(0))
            fill_tags(b)
            taggot_ref[b] = tag_ref[b]
            fill(b, None, 0)
    for cut in range(1, CUTS):
        fill(b, None, cut)
    arrive(batch_copies(0))
    begin(batch_copies(1))

    picks = pick_of_slots(taggot_ref, depth, flag_at, capacity)

    slots = slots_of_tags(taggot_ref, depth, flag_at, capacity)

    def compact(cut):
        columns = pl.ds(cut * wide, wide)
        for c in range(capacity):
            hits = [jnp.where(place == c, live, 0) for place, live in slots]
            k = sum(n * hits[n] for n in range(c, len(slots)))
            there = sum(hits[c:]).astype(F32)
            part_ref[c, :, columns] = (got_refs[cut][k].astype(F32) * there).astype(BF16)
        begin(row_copies(cut, 0))

    compact(0)
    first_gather.advance(1, 1, 0)
    arrive(batch_copies(1))
    for cut in range(2, CUTS):
        begin(batch_copies(cut))
        compact(cut - 1)
        if cut == 2:
            first_gather.advance(1, 2)
        arrive(batch_copies(cut))
    compact(CUTS - 1)
    first_gather.advance(2, 1, 0, 2)
    second_gather.start()
    for r in range(1, own_rows):
        for cut in range(CUTS):
            begin(row_copies(cut, r))
    for c in range(capacity):
        total = jnp.zeros((1, tags_ref.shape[1]), F32)
        for k in range(c, len(picks)):
            total += picks[k][c] * taggot_ref[k // depth, k % depth : k % depth + 1]
        taglocal_ref[c, 0:1] = total
    for i in range(own_rows):
        x_ref[i, mine] = part_ref[z * own_rows + i]
    own_ref[...] = jnp.zeros_like(own_ref)
    for i in range(own_rows):
        own_ref[i : i + 1] = taglocal_ref[z * own_rows + i, 0:1]
    got_tags_ref[...] = taggot_ref[...]

    first_gather.advance(3, 1, 0, 2)
    arrive(vec_copies())
    vecgot_ref[z] = vec_ref[...]
    vecs_ref[...] = vecgot_ref[...]
    for copy in local_copies():
        copy.wait()
    keep = [
        pltpu.make_async_copy(x_ref, x_out, local_sem.at[3]),
        pltpu.make_async_copy(wa_ref, wa_out, local_sem.at[4]),
    ]

    def rows_here(r):
        for cut in range(CUTS):
            arrive(row_copies(cut, r))

    rows_here(0)
    seg_rows = own_ref[:, head:]
    seg_cols = seg_rows.T
    def forward_early():
        arrive(third_gather.early_copies(0))
        begin(third_gather.early_copies(1))

    late = {
        (0, 1): ((first_gather.done, 1),),
        (0, 2): ((first_gather.done, 0), (second_gather.advance, 1, 1, 0)),
        (0, 3): ((first_gather.done, 2), (second_gather.advance, 1, 2)),
        (1, 0): ((second_gather.advance, 2, 2),),
        (1, 1): ((second_gather.advance, 3, 1, 0),),
        (1, 2): ((second_gather.advance, 3, 2), (forward_early,)),
    }

    for r in range(own_rows):
        if r == 1:
            second_gather.advance(2, 1, 0)
            begin(third_gather.early_copies(0))
            for n in range(1, own_rows):
                rows_here(n)
            begin(keep)
        mask_ref[...] = jnp.where(seg_cols[:, r : r + 1] == seg_rows[r : r + 1], 0.0, NEG)
        acc_ref[...] = jnp.zeros_like(acc_ref)

        def one_group(i, _):
            m = chunk_of(at, model_size - 1 - i)
            for step in range(model_size):
                if (r, step) in late:
                    @pl.when(i == step)
                    def _():
                        for action, *args in late[r, step]:
                            action(*args)

            bias = vecgot_ref[m].T[: 3 * group_dim, 0:1]
            low = (mm(wa_ref[m, : 3 * group_dim, :], x_ref[r], NT) + bias).astype(BF16)
            qkv_ref[r, m] = low
            for j in range(group_dim // HEAD_DIM):
                rows = slice(j * HEAD_DIM, (j + 1) * HEAD_DIM)
                q_t = low[rows] * HEAD_DIM ** (-0.5)
                k_t = low[group_dim + rows.start : group_dim + rows.stop]
                v_t = low[2 * group_dim + rows.start : 2 * group_dim + rows.stop]
                scores = mm(k_t, q_t, TN) + mask_ref[...]
                top = jnp.max(scores, axis=0, keepdims=True)
                terms = jnp.exp(scores - top)
                total = jnp.sum(terms, axis=0, keepdims=True)
                ctx_t = mm(v_t, terms.astype(BF16)) / total
                ctx_ref[r, m, rows, :] = ctx_t.astype(BF16)
                lse_ref[r, m, j : j + 1, :] = top + jnp.log(total)
            acc_ref[...] += mm(ctx_ref[r, m], wa_ref[m, 3 * group_dim :, :], TN)
            return 0

        lax.fori_loop(0, model_size, one_group, 0)
        xhat, rstd = norm_parts(x_ref[r].astype(F32) + (acc_ref[...] + bout_ref[...].reshape(1, dim)))
        xhat_ref[r] = xhat
        rstd_ref[r] = rstd

    second_gather.done(0, 1, 2)
    arrive(third_gather.early_copies(1))
    for copy in keep:
        copy.wait()
    for gather in gathers:
        gather.sent()
    sent(third_gather.early_copies(0) + third_gather.early_copies(1))
    sent(vec_copies())
    for cut in range(CUTS):
        sent(batch_copies(cut))
        for r in range(own_rows):
            sent(row_copies(cut, r))


def enter(exit_flag, target, rows_in, seg, labels, weights, w_qkv, w_out, b_qv, b_up, b_out, w_b, w_c,
          own_rows, batch_size, model_size):
    row_count, token_part, dim = rows_in.shape
    seq = token_part * model_size
    capacity = own_rows * model_size
    depth = (capacity + batch_size - 1) // batch_size
    group_dim = dim // model_size
    pairs = labels.shape[1]
    tag_wide = 128 + seq
    smem = pl.BlockSpec(memory_space=pltpu.SMEM)
    vmem = pl.BlockSpec(memory_space=pltpu.VMEM)
    hbm = pl.BlockSpec(memory_space=pl.ANY)
    full = jax.ShapeDtypeStruct((model_size, dim, dim), BF16)
    f32 = lambda *shape: jax.ShapeDtypeStruct(shape, F32)
    low = lambda *shape: jax.ShapeDtypeStruct(shape, BF16)
    moves = (CUTS + 1) * (batch_size + model_size) + CUTS * own_rows * model_size
    return pl.pallas_call(
        functools.partial(enter_kernel, depth, pairs),
        in_specs=[smem, smem] + [vmem] * 9 + [hbm, hbm],
        out_specs=[vmem, vmem, vmem, hbm, hbm, hbm, hbm] + [vmem] * 5,
        out_shape=(
            f32(8, tag_wide),
            f32(batch_size, 8, tag_wide),
            f32(model_size, 8, dim),
            low(own_rows, seq, dim),
            full,
            full,
            low(3, 2, dim // 16, dim),
            low(own_rows, model_size, 3 * group_dim, seq),
            low(own_rows, model_size, group_dim, seq),
            f32(own_rows, model_size, group_dim // HEAD_DIM, seq),
            f32(own_rows, seq, dim),
            f32(own_rows, seq, 1),
        ),
        scratch_shapes=[
            pltpu.VMEM((-(-row_count // 8) * 8, tag_wide), F32),
            pltpu.VMEM((8, dim), F32),
            pltpu.VMEM((dim, dim), BF16),
            pltpu.VMEM((batch_size * depth, token_part, dim), BF16),
            pltpu.VMEM((capacity, token_part, dim), BF16),
            pltpu.VMEM((own_rows, seq, dim), BF16),
            pltpu.VMEM((model_size, dim, dim), BF16),
            pltpu.VMEM((batch_size, 8, tag_wide), F32),
            pltpu.VMEM((batch_size, 8, tag_wide), F32),
            pltpu.VMEM((capacity, 8, tag_wide), F32),
            pltpu.VMEM((model_size, 8, dim), F32),
            pltpu.VMEM((seq, seq), F32),
            pltpu.VMEM((seq, dim), F32),
            pltpu.SemaphoreType.DMA((3, GATHER_SEMS)),
            pltpu.SemaphoreType.DMA((3, GATHER_SEMS)),
            pltpu.SemaphoreType.DMA((moves,)),
            pltpu.SemaphoreType.DMA((moves,)),
            pltpu.SemaphoreType.DMA((5,)),
            *[pltpu.VMEM((batch_size * depth, token_part, dim // CUTS), BF16) for _ in range(CUTS)],
        ],
        compiler_params=pltpu.CompilerParams(
            vmem_limit_bytes=VMEM_MOST, collective_id=0, has_side_effects=True
        ),
        name="enter",
    )(
        exit_flag, target, rows_in, seg, labels.T, weights.T, jnp.transpose(w_qkv, (0, 2, 1)), w_out, b_qv, b_up, b_out,
        w_b, w_c,
    )


def leave_kernel(
    depth, pairs,
    exit_ref, target_ref, tags_ref, own_ref, x_ref, gres_hbm, wa_ref, qkv_hbm, ctx_ref, lse_ref,
    dwb_hbm, ownc_ref, hand_ref, pack_ref,
    rows_ref, mats_ref, sums_ref, bias_ref,
    work_ref, acc_ref, mask_ref, p_ref, s_ref, xflip_ref, gflip_ref, dx_ref, dwa_ref,
    own_half, *rest,
):
    parts_a, parts_b, parts_c, rest = rest[:7], rest[7:14], rest[14:19], rest[19:]
    (
        small_acc, small_got, small_z, bias_acc, bias_got, bias_z, back_ref, back_got,
        msend, mrecv, ssend, srecv, bsend, brecv, rsend, rrecv, local_sem, *mine_refs,
    ) = rest
    row_count, seq, dim = x_ref.shape
    model_size = wa_ref.shape[0]
    batch_size = tags_ref.shape[0]
    group_dim = ctx_ref.shape[2]
    token_part = seq // model_size
    capacity = row_count * model_size
    others = model_size - 1
    at = mesh_place()
    b, z, lo, hi = at["b"], at["z"], at["lo"], at["hi"]
    far, twin, side = at["far"], at["twin"], at["side"]

    def shard(i):
        return {"mp": (z + i) % model_size}

    first = Reduce(at, model_size, dwb_hbm, own_half, *parts_b, mats_ref.at[1], msend.at[1], mrecv.at[1])
    second = Reduce(at, model_size, dwa_ref, dwa_ref.at[:, :, lo], *parts_a, mats_ref.at[0], msend.at[0], mrecv.at[0], 2, True)
    third = Finish(at, model_size, ownc_ref, hand_ref, *parts_c, mats_ref.at[2], msend.at[2], mrecv.at[2])

    def small_copies(stage):
        def one(slot, src, dst, device):
            return remote(src, dst, ssend.at[slot], srecv.at[slot], device)

        if stage == 0:
            return [one(0, pack_ref.at[1 - lo], small_got.at[0], twin)]
        if stage < 3:
            return [one(stage, small_acc.at[stage - 1], small_got.at[stage], (far, side)[stage - 1])]
        if stage == 3:
            return [
                one(2 + i, small_acc.at[2, (z + i) % model_size], small_z.at[i - 1], shard(i))
                for i in range(1, model_size)
            ]
        if stage == 4:
            return [
                one(2 + others + i, sums_ref.at[lo, z], sums_ref.at[lo, z], shard(i))
                for i in range(1, model_size)
            ]
        return [one(3 + 2 * others, sums_ref.at[lo], sums_ref.at[lo], twin)]

    def bias_copies(stage):
        def one(slot, src, dst, device):
            return remote(src, dst, bsend.at[slot], brecv.at[slot], device)

        if stage < 3:
            return [one(stage, bias_acc.at[stage], bias_got.at[stage], (twin, far, side)[stage])]
        return [
            one(2 + i, bias_acc.at[3, (z + i) % model_size], bias_z.at[i - 1], shard(i))
            for i in range(1, model_size)
        ]

    wide = dim // CUTS

    def row_copies(r, cut):
        columns = pl.ds(cut * wide, wide)
        first = (r * CUTS + cut) * others - 1
        return [
            remote(
                dx_ref.at[r, pl.ds(pl.multiple_of((z + i) % model_size * token_part, 128), token_part), columns],
                mine_refs[cut].at[z * row_count + r],
                rsend.at[first + i], rrecv.at[first + i], shard(i),
            )
            for i in range(1, model_size)
        ]

    def batch_copies(cut):
        columns = pl.ds(cut * wide, wide)
        first = row_count * CUTS * others + cut * (batch_size - 1) - 1
        copies = []
        for j in range(1, batch_size):
            t = (b + j) % batch_size
            copies.append(remote(
                back_ref.at[pl.ds(t * depth, depth), :, columns],
                back_got.at[pl.ds(b * depth, depth), :, columns],
                rsend.at[first + j], rrecv.at[first + j], {"batch": t},
            ))
        return copies

    def local_copies():
        return [
            pltpu.make_async_copy(dwb_hbm.at[:, :, lo], own_half, local_sem.at[0]),
        ]

    def inputs():
        return [
            pltpu.make_async_copy(qkv_hbm, work_ref, local_sem.at[2]),
            pltpu.make_async_copy(gres_hbm, acc_ref, local_sem.at[3]),
        ]

    def small_step(stage):
        arrive(small_copies(stage))
        if stage == 0:
            small_acc[0] = pack_ref[lo] + small_got[0]
        if stage in (1, 2):
            small_acc[stage] = small_acc[stage - 1] + small_got[stage]
        if stage == 3:
            total = small_acc[2, z]
            for i in range(others):
                total += small_z[i]
            sums_ref[lo, z] = total
        if stage < 5:
            begin(small_copies(stage + 1))

    def bias_step(stage):
        arrive(bias_copies(stage))
        if stage < 3:
            bias_acc[stage + 1] = bias_acc[stage] + bias_got[stage]
            begin(bias_copies(stage + 1))
        else:
            total = bias_acc[3, z]
            for i in range(others):
                total += bias_z[i]
            bias_ref[...] = total

    begin(inputs())
    begin(local_copies())
    greet(at, batch_size, model_size)
    begin(small_copies(0))
    third.start()
    for i in range(model_size):
        first.start(i)
    seg_rows = own_ref[:, own_ref.shape[1] - seq :]
    seg_cols = seg_rows.T
    for copy in inputs() + local_copies():
        copy.wait()

    steps = {
        0: [],
        1: [(small_step, 0), (third.after_one,), (first.after_core, 0)],
        2: [(first.after_core, 1), (first.after_one, 0)],
        3: [(first.after_core, 2), (first.after_one, 1), (first.after_two, 0), (small_step, 1), (third.after_two,)],
        4: [(first.after_core, 3), (first.after_one, 2), (first.after_two, 1), (small_step, 2)],
        5: [(first.after_one, 3), (first.after_two, 2), (small_step, 3), (third.after_three,)],
        6: [(second.after_core, 0), (first.after_two, 3), (small_step, 4)],
        7: [(second.after_core, 1), (second.after_one, 0), (first.after_three,)],
    }

    def weight_grads(i):
        m, rows_y = chunk_of(at, i), dim // 2

        def one(y, _):
            part = pl.ds(pl.multiple_of(y * rows_y, 128), rows_y)
            left, right = 0.0, 0.0
            for q in range(row_count):
                cols = slice(q * seq, (q + 1) * seq)
                left += mm(xflip_ref[part, cols], work_ref[q, m], NT)
                right += mm(gflip_ref[part, cols], ctx_ref[q, m], NT)
            shape = dwa_ref.shape[2:-1]
            dwa_ref[m, y, :, :, :, :, : 3 * group_dim] = left.astype(BF16).reshape(*shape, 3 * group_dim)
            dwa_ref[m, y, :, :, :, :, 3 * group_dim :] = right.astype(BF16).reshape(*shape, group_dim)
            return 0

        lax.fori_loop(0, 2, one, 0)

    for r in range(row_count):
        mask_ref[...] = jnp.where(seg_cols[:, r : r + 1] == seg_rows[r : r + 1], 0.0, NEG)
        grad_low = acc_ref[r].astype(BF16)
        columns = slice(r * seq, (r + 1) * seq)
        gflip_ref[:, columns] = grad_low.T
        xflip_ref[:, columns] = x_ref[r].T

        def one_group(i, _):
            if r == row_count - 1:
                @pl.when(i > 0)
                def _():
                    weight_grads(i - 1)

            for step in range(model_size):
                @pl.when(i == step)
                def _():
                    if r == row_count - 1 and step > 0:
                        second.start(step - 1)
                    for action, *args in steps[r * model_size + step]:
                        action(*args)

            m = chunk_of(at, i)
            grad_ctx = mm(wa_ref[m, 3 * group_dim :, :], grad_low, NT).astype(BF16)

            def store(rows, value):
                work_ref[r, m, rows, :] = value

            backward_group(
                grad_ctx, lambda rows: ctx_ref[r, m, rows, :], lambda rows: work_ref[r, m, rows, :], store,
                mask_ref, lambda j: lse_ref[r, m, j : j + 1, :], group_dim, p_ref, s_ref,
            )
            grads = work_ref[r, m]
            found = mm(jnp.ones((8, seq), BF16), grads, NT)
            if r == 0:
                bias_acc[0, m] = found
            else:
                bias_acc[0, m] = bias_acc[0, m] + found
            acc_ref[r] = acc_ref[r] + mm(grads, wa_ref[m, : 3 * group_dim, :], TN)
            return 0

        lax.fori_loop(0, model_size, one_group, 0)
        dx_ref[r] = acc_ref[r].astype(BF16)
        for cut in range(CUTS if r < row_count - 1 else 2):
            begin(row_copies(r, cut))

    weight_grads(model_size - 1)
    second.start(model_size - 1)
    for r in range(row_count):
        for cut in range(CUTS):
            part = pl.ds(pl.multiple_of(z * token_part, 128), token_part)
            mine_refs[cut][z * row_count + r] = dx_ref[r, part, cut * wide : (cut + 1) * wide]
    second.after_core(2)
    slots = slots_of_tags(tags_ref, depth, 2 * pairs, capacity)

    def give(cut):
        columns = pl.ds(cut * wide, wide)
        for k, (place, live) in enumerate(slots):
            found = mine_refs[cut][place].astype(F32) * live.astype(F32)
            back_ref[k, :, columns] = found.astype(BF16)
        begin(batch_copies(cut))

    def returned(cut):
        for r in range(row_count):
            arrive(row_copies(r, cut))
        if cut + 2 < CUTS:
            begin(row_copies(row_count - 1, cut + 2))
        give(cut)

    returned(0)
    second.after_core(3)
    second.after_one(1)
    second.after_two(0)
    begin(bias_copies(0))
    returned(1)
    second.after_one(2)
    second.after_two(1)
    first.after_four()
    returned(2)
    second.after_one(3)
    second.after_two(2)
    bias_step(0)
    small_step(5)
    own_slots = pl.ds(b * depth, depth)
    back_got[own_slots] = back_ref[own_slots]
    bias_step(1)
    second.after_two(3)
    second.after_three()
    bias_step(2)
    third.done()
    bias_step(3)
    flat = slot_of_rows(exit_ref, target_ref, depth)
    for cut in range(CUTS):
        arrive(batch_copies(cut))

    for r in range(rows_ref.shape[0]):
        k = jnp.minimum(jnp.maximum(flat[r], 0), batch_size * depth - 1)
        alive = jnp.where(flat[r] >= 0, 1.0, 0.0)
        rows_ref[r] = (back_got[k].astype(F32) * alive).astype(BF16)
    for reducer in (first, second):
        reducer.done()
        reducer.sent()
    third.sent()
    for stage in range(6):
        sent(small_copies(stage))
    for stage in range(4):
        sent(bias_copies(stage))
    for cut in range(CUTS):
        for r in range(row_count):
            sent(row_copies(r, cut))
        sent(batch_copies(cut))


def leave(exit_flag, target, tags, own, x, gres, w_a, qkv, ctx, lse, d_wb, mat_c, hand, pack, row_total, batch_size, pairs):
    rows, seq, dim = x.shape
    model_size = w_a.shape[0]
    group_dim = dim // model_size
    token_part = seq // model_size
    capacity = rows * model_size
    depth = (capacity + batch_size - 1) // batch_size
    slots = batch_size * depth
    piece = dim // 16
    others = model_size - 1
    grid_shape = (model_size, 2, 2, PARTS, 2, piece, dim)
    pack_shape = (2, model_size, pack.shape[0] // (2 * model_size), pack.shape[1])
    smem = pl.BlockSpec(memory_space=pltpu.SMEM)
    vmem = pl.BlockSpec(memory_space=pltpu.VMEM)
    hbm = pl.BlockSpec(memory_space=pl.ANY)
    dma = pltpu.SemaphoreType.DMA
    low = lambda *shape: pltpu.VMEM(shape, BF16)
    f32 = lambda *shape: pltpu.VMEM(shape, F32)
    row_moves = CUTS * (rows * others + batch_size - 1)
    return pl.pallas_call(
        functools.partial(leave_kernel, depth, pairs),
        in_specs=[smem, smem, vmem, vmem, vmem, hbm, vmem, hbm, vmem, vmem, hbm, vmem, vmem, vmem],
        out_specs=[vmem, vmem, vmem, vmem],
        out_shape=(
            jax.ShapeDtypeStruct((row_total, token_part, dim), BF16),
            jax.ShapeDtypeStruct((3,) + grid_shape[2:], BF16),
            jax.ShapeDtypeStruct(pack_shape, F32),
            jax.ShapeDtypeStruct((8, 3 * group_dim), F32),
        ),
        scratch_shapes=[
            low(rows, model_size, 3 * group_dim, seq),
            f32(rows, seq, dim),
            f32(seq, seq),
            low(2, seq, seq),
            low(2, seq, seq),
            low(dim, rows * seq),
            low(dim, rows * seq),
            low(rows, seq, dim),
            low(*grid_shape),
            low(model_size, 2, PARTS, 2, piece, dim),
            *reduce_scratch(model_size, piece, dim),
            *reduce_scratch(model_size, piece, dim),
            low(2, piece, dim),
            low(2, piece, dim),
            low(piece, dim),
            low(piece, dim),
            low(PARTS, piece, dim),
            f32(3, *pack_shape[1:]),
            f32(3, *pack_shape[1:]),
            f32(others, *pack_shape[2:]),
            f32(4, model_size, 8, 3 * group_dim),
            f32(3, model_size, 8, 3 * group_dim),
            f32(others, 8, 3 * group_dim),
            low(slots, token_part, dim),
            low(slots, token_part, dim),
            dma((3, REDUCE_SEMS)),
            dma((3, REDUCE_SEMS)),
            dma((4 + 2 * others,)),
            dma((4 + 2 * others,)),
            dma((3 + others,)),
            dma((3 + others,)),
            dma((row_moves,)),
            dma((row_moves,)),
            dma((4,)),
            *[low(capacity, token_part, dim // CUTS) for _ in range(CUTS)],
        ],
        compiler_params=pltpu.CompilerParams(
            vmem_limit_bytes=VMEM_MOST, collective_id=2, has_side_effects=True
        ),
        name="leave",
    )(
        exit_flag, target, tags, own, x, gres, w_a, qkv, ctx, lse,
        d_wb.reshape(grid_shape), mat_c, hand, pack.reshape(pack_shape),
    )


def finish_kernel(
    classes, mats_ref, sums_ref, bias_ref,
    gqkv_ref, gbqv_ref, gout_ref, gbout_ref, ggain_ref, gshift_ref, gup_ref, gbup_ref, gdown_ref, gbdown_ref,
    gsw1_ref, gsbias_ref, gquery_ref, gsw2_ref, gsw3_ref, gsb3_ref,
):
    dim, width = gsw1_ref.shape
    group_dim = gout_ref.shape[0]
    b, z = lax.axis_index("batch"), lax.axis_index("mp")
    w2_at, w3_at, small_at, vec_at, bup_at = pack_places(dim, width)
    blocks = dim // width

    def vector(first, row):
        return jnp.concatenate([sums_ref[first + j * 8 + row : first + j * 8 + row + 1] for j in range(blocks)], axis=1)

    def share(value, parts):
        size = value.shape[1] // parts
        return sum(jnp.where(b == i, 1.0, 0.0) * value[:, i * size : (i + 1) * size] for i in range(parts))

    parts = dim // gbup_ref.shape[-1]
    flipped = mats_ref[0].astype(F32).T
    for j in range(3):
        gqkv_ref[j] = flipped[j * group_dim : (j + 1) * group_dim]
    gout_ref[...] = flipped[3 * group_dim :]
    gup_ref[...] = mats_ref[1].astype(F32)
    gdown_ref[...] = mats_ref[2].astype(F32).T
    for n in range(2):
        gbqv_ref[n : n + 1] = share(bias_ref[0:1, 2 * n * group_dim : (2 * n + 1) * group_dim], parts)
    gbout_ref[...] = (vector(vec_at.start, 5)).reshape(dim)
    for n in range(2):
        ggain_ref[n : n + 1] = vector(vec_at.start, n)
        gshift_ref[n : n + 1] = vector(vec_at.start, 2 + n)
    gbdown_ref[...] = (vector(vec_at.start, 4)).reshape(dim)
    ups = [vector(bup_at.start, m) for m in range(dim // group_dim)]
    gbup_ref[...] = (share(sum(jnp.where(z == m, 1.0, 0.0) * ups[m] for m in range(len(ups))), parts)).reshape(gbup_ref.shape[0])
    for j in range(blocks):
        gsw1_ref[j * width : (j + 1) * width] = sums_ref[j * width : (j + 1) * width].T
    gsbias_ref[...] = sums_ref[small_at.start : small_at.start + 2]
    gquery_ref[...] = (sums_ref[small_at.start + 2 : small_at.start + 3]).reshape(width)
    gsb3_ref[...] = (sums_ref[small_at.start + 3 : small_at.start + 4][:, :classes]).reshape(classes)
    gsw2_ref[...] = sums_ref[w2_at]
    gsw3_ref[...] = sums_ref[w3_at][:classes]


def finish(mats, sums, bias, model_size, classes):
    depth, dim = mats.shape[1:]
    width = sums.shape[1]
    group_dim = dim // model_size
    batch_size = dim // depth
    f32 = lambda *shape: jax.ShapeDtypeStruct(shape, F32)
    return pl.pallas_call(
        functools.partial(finish_kernel, classes),
        out_shape=(
            f32(3, group_dim, depth),
            f32(2, group_dim // batch_size),
            f32(group_dim, depth),
            f32(dim),
            f32(2, dim),
            f32(2, dim),
            f32(depth, dim),
            f32(depth),
            f32(dim, depth),
            f32(dim),
            f32(dim, width),
            f32(2, width),
            f32(width),
            f32(width, width),
            f32(classes, width),
            f32(classes),
        ),
        compiler_params=pltpu.CompilerParams(vmem_limit_bytes=VMEM_MOST),
        name="finish",
    )(mats, sums, bias)


def rows_back(grad_x, exit_flag, target, live, slot_depth):
    batch_size, model_size = lax.axis_size("batch"), lax.axis_size("mp")
    own_rows, seq, dim = grad_x.shape
    row_count = exit_flag.shape[0]
    capacity, slot_count = own_rows * model_size, batch_size * slot_depth
    alive_rows = 1 - exit_flag > 0
    same_goal = (target[:, None] == target[None, :]) & alive_rows[:, None] & alive_rows[None, :]
    row_order = jnp.arange(row_count, dtype=jnp.int32)
    slot_in = jnp.sum(
        (same_goal & (row_order[None, :] < row_order[:, None])).astype(jnp.int32), axis=1
    )
    flat_slot = target * slot_depth + slot_in
    send_low = (
        (jnp.arange(slot_count, dtype=jnp.int32)[:, None] == flat_slot[None, :]) & alive_rows[None, :]
    ).astype(BF16)
    live_flat = live.reshape(-1)
    position = jnp.cumsum(live_flat.astype(jnp.int32)) - 1
    pick_low = (
        (jnp.arange(capacity, dtype=jnp.int32)[:, None] == position[None, :]) & (live_flat[None, :] > 0)
    ).astype(BF16)
    mine = lax.all_to_all(grad_x, "mp", split_axis=1, concat_axis=0, tiled=True)
    back = jnp.einsum("ck,csd->ksd", pick_low, mine, preferred_element_type=F32).astype(BF16)
    back = back.reshape((batch_size, slot_depth) + back.shape[1:])
    got = lax.all_to_all(back, "batch", split_axis=0, concat_axis=0, tiled=True)
    got = got.reshape((slot_count,) + got.shape[2:])
    return jnp.einsum("kr,ksd->rsd", send_low, got, preferred_element_type=F32).astype(BF16)


def matrix_sums(grads):
    sums = []
    for grad in grads:
        part = lax.psum_scatter(grad, "mp", scatter_dimension=0, tiled=True)[0]
        part = lax.psum_scatter(part, "batch", scatter_dimension=0, tiled=True)
        sums.append(lax.psum(part, "grp"))
    return sums


def on_device(
    rows_in, segment_ids, pair_labels, pair_mask, exit_flag, target, cot_out,
    w_qkv, b_qv, w_out, b_out, ln_gain, ln_bias, w_up, b_up, w_down, b_down,
    s_w1, s_bias, s_query, s_w2, s_w3, s_b3,
):
    batch_size = lax.axis_size("batch")
    model_size = lax.axis_size("mp")
    row_count, _, model_dim = rows_in.shape
    own_rows = cot_out.shape[0]
    capacity = own_rows * model_size
    slot_depth = (capacity + batch_size - 1) // batch_size
    pair_count = pair_labels.shape[1]
    my_mp = lax.axis_index("mp")
    own, got_tags, vecs, rows_own, w_a, w_b, early, qkv, ctx, lse, xhat_one, rstd_one = enter(
        exit_flag, target, rows_in, segment_ids, pair_labels, pair_mask, w_qkv, w_out, b_qv, b_up, b_out,
        w_up, w_down, own_rows, batch_size, model_size,
    )
    scatter = batch_size == 2
    mixed_out, grad_resid, d_wb, mat_c, hand, pack = ffn_both(
        xhat_one, rstd_one, ln_gain, ln_bias, w_b, w_down, early, vecs, b_down, cot_out, own, pair_count, scatter,
        s_w1, s_bias, s_query, s_w2, s_w3, s_b3,
    )
    if scatter:
        grad_rows, mats, sums, bias_sum = leave(
            exit_flag, target, got_tags, own, rows_own, grad_resid, w_a, qkv, ctx, lse, d_wb, mat_c, hand, pack,
            row_count, batch_size, pair_count,
        )
        mats = mats.reshape(3, model_dim // batch_size, model_dim)
        sums = sums.reshape(pack.shape)
    else:
        grad_x, d_wa, bias_part = attn_backward(rows_own, grad_resid, w_a, qkv, ctx, lse, own)
        grad_rows = rows_back(grad_x, exit_flag, target, got_tags[:, :slot_depth, 2 * pair_count], slot_depth)
        whole = (model_size, model_dim, model_dim)
        mats = matrix_sums((d_wa, d_wb.reshape(whole), mat_c.reshape(whole)))
        sums, bias_sum = lax.psum((pack, bias_part[:, 0]), ("grp", "batch", "mp"))
        bias_sum = lax.dynamic_index_in_dim(bias_sum, my_mp, 0)
        mats = jnp.stack(mats)

    (
        g_wqkv, g_bqv, g_wout, g_bout, g_gain, g_shift, g_wup, g_bup, g_wdown, g_bdown,
        g_sw1, g_sbias, g_query, g_sw2, g_sw3, g_sb3,
    ) = finish(mats, sums, bias_sum, model_size, s_w3.shape[1])
    return (
        mixed_out, grad_rows, jnp.transpose(g_wqkv, (0, 2, 1)), g_bqv, g_wout, g_bout, g_gain, g_shift, g_wup,
        g_bup, g_wdown, g_bdown, g_sw1, g_sbias, g_query, g_sw2, g_sw3.T, g_sb3,
    )


def solution(mesh):
    return jax.shard_map(
        on_device,
        mesh=mesh,
        in_specs=(
            P(("grp", "batch"), "mp", None),
            P(("grp", "batch"), None),
            P(("grp", "batch"), None),
            P(("grp", "batch"), None),
            P(("grp", "batch")),
            P(("grp", "batch")),
            P(("grp", "batch", "mp"), None, None),
            P(None, None, "mp"),
            P(None, "mp"),
            P("mp", None),
            P(),
            P(),
            P(),
            P(None, "mp"),
            P("mp"),
            P("mp", None),
            P(),
            P(),
            P(),
            P(),
            P(),
            P(),
            P(),
        ),
        out_specs=(
            P(("grp", "batch", "mp"), None, None),
            P(("grp", "batch"), "mp", None),
            P(None, "batch", "mp"),
            P(None, ("mp", "batch")),
            P("mp", "batch"),
            P(),
            P(),
            P(),
            P("batch", "mp"),
            P(("mp", "batch")),
            P("mp", "batch"),
            P(),
            P(),
            P(),
            P(),
            P(),
            P(),
            P(),
        ),
        check_vma=False,
    )
```

time: 1490 us -> 292 us (0.20)
  waiting for transfers between devices: 1010 us -> 0 us
  Pallas kernels: 0 us -> 286 us
  matrix products: 220 us -> 0 us
  other arithmetic: 104 us -> 0 us
  blocking collectives: 62.1 us -> 0 us
  local copies, waits for them, and re-layouts: 62.7 us -> 2.98 us
  starting transfers between devices: 16.5 us -> 0 us
    all_gather x4 -> x0, waiting for transfers between devices: 447 us -> none  [the longest x1 116 us: on_device(): hidden_all = lax.all_gather(hidden_low, 'mp', axis=0, tiled=True)]
    reduce_scatter x5 -> x0, waiting for transfers between devices: 432 us -> none  [the longest x1 111 us: on_device(): lax.psum_scatter(grad_input.astype(jnp.bfloat16), 'mp', scatter_dimension...]
    pallas_call x0 -> x4, Pallas kernels: none -> 286 us  [the longest x1 121 us: leave(): pl.pallas_call(functools.partial(leave_kernel, depth, pairs), in_specs=[s...]
    dot_general x90 -> x0, matrix products: 220 us -> none  [the longest x16 31.2 us: score_rows(): jnp.einsum('qhe,khe->hqk', queries, key_rows, preferred_element_type=jnp....]
    psum x2 -> x0, waiting for transfers between devices: 105 us -> none  [the longest x1 105 us: on_device(): lax.psum((g_bout, jnp.stack([g_gain_one, g_gain_two]), jnp.stack([g_shift...]
    convert_element_type x22 -> x0, other arithmetic: 58.2 us -> none  [the longest x1 29.9 us: on_device(): active_low = active.astype(jnp.bfloat16)]
    psum x2 -> x0, blocking collectives: 48.3 us -> none  [the longest x1 41 us: on_device(): lax.psum((g_bout, jnp.stack([g_gain_one, g_gain_two]), jnp.stack([g_shift...]
    reduce_sum x25 -> x0, other arithmetic: 28.9 us -> none  [the longest x4 10.7 us: layer_norm(): center = resid_in - jnp.mean(resid_in, axis=-1, keepdims=True)]
  transfers between devices with their start and end apart: 19 -> 0, of which waited for: 11 -> 0; matrix products, arithmetic and copies ran while one was open for 14% -> 0% of each run, Pallas kernels for 0% -> 0%
where the time goes in v1:
time: 292 us; the launch traced here: 289 us
  Pallas kernels  286 us (98%)
  local copies, waits for them, and re-layouts  2.98 us (1%)
    pallas_call x1, Pallas kernels, leave(): pl.pallas_call(functools.partial(leave_kernel, depth, pairs), in_specs=[s...  121 us
    pallas_call x1, Pallas kernels, enter(): pl.pallas_call(functools.partial(enter_kernel, depth, pairs), in_specs=[s...  83.3 us
    pallas_call x1, Pallas kernels, ffn_both(): pl.pallas_call(functools.partial(ffn_kernel, classes, pairs, scatter), in...  77.9 us

profile of v1, /device:TPU:1, one launch (start us, length us, event | category | flops | bytes accessed | tf_op | source)
XLA Modules:
  0.0 289.4 jit_solution(10416984356789088765)
XLA Ops:
  0.7 83.3 %enter.1 = (f32[8,640]{1,0:T(8,128)}, f32[2,8,640]{2,1,0:T(8,128)}, f32[4,8,768]{2,1,0:T(8,128)}, bf16[2,512,768]{2,1,0:T(8,128)(2,1)}, bf16[4,768,768]{2,1,0:T(...) custom-call(s32[7]{0:T(128)} %exit_ref.3, ...), custom_call_target="tpu_custom_call" | custom-call | tf_op jit(solution)/shard_map/enter/pallas_call | solution.py:1184
  84.0 77.9 %ffn_both.1 = (bf16[2,512,768]{2,1,0:T(8,128)(2,1)}, f32[2,512,768]{2,1,0:T(8,128)}, bf16[4,2,2,2,2,48,768]{6,5,4,3,2,1,0:T(8,128)(2,1)}, bf16[2,2,2,48,768]{4,3...) custom-call(f32[2,512,768]{2,1,0:T(8,128)} %get-tuple-element.56.xhat1_ref, ...), custom_call_target="tpu_custom_call" | custom-call | tf_op jit(solution)/shard_map/ffn_both/pallas_call | solution.py:728
  161.9 120.5 %leave.1 = (bf16[7,128,768]{2,1,0:T(8,128)(2,1)}, bf16[3,2,2,2,48,768]{5,4,3,2,1,0:T(8,128)(2,1)}, f32[2,4,128,128]{3,2,1,0:T(8,128)}, f32[8,576]{1,0:T(8,128)}) custom-call(s32[7]{0:T(128)} %exit_ref.3, s32[7]{0:T(128)} %target_ref.3, f32[2,8,640]{2,1,0:T(8,128)} %get-tuple-element.63.tags_ref, f32[8,640]{1,0:T(8,128)} %get-tuple-element.61.own_ref, ...), custom_call_target="tpu_custom_call" | custom-call | tf_op jit(solution)/shard_map/leave/pallas_call | solution.py:1529
  282.4 0.0 copy-start
  282.4 4.0 %finish.1 = (f32[3,192,384]{2,1,0:T(8,128)}, f32[2,96]{1,0:T(2,128)}, f32[192,384]{1,0:T(8,128)}, f32[768]{0:T(1024)}, f32[2,768]{1,0:T(2,128)}, /*index=5*/f32[...) custom-call(bf16[3,384,768]{2,1,0:T(8,128)(2,1)} %bitcast.9, ...), custom_call_target="tpu_custom_call" | custom-call | tf_op jit(solution)/shard_map/finish/pallas_call | solution.py:1635
  286.4 0.0 copy-done
  286.4 0.0 copy-start.1
  286.4 1.1 copy.43
  287.6 0.8 copy-done.1
  288.3 1.1 copy.44
Async XLA Ops:
  282.4 4.0 %copy-start = (bf16[2,512,768]{2,1,0:T(8,128)(2,1)S(1)}, bf16[2,512,768]{2,1,0:T(8,128)(2,1)}, u32[]{:S(2)}) copy-start(bf16[2,512,768]{2,1,0:T(8,128)(2,1)} %get-tuple-element.112) | copy-start | bytes 4718596
  286.4 1.9 copy-start.1

commit v2 on v1

--- a/solution.py
+++ b/solution.py
@@ -89,9 +89,6 @@
 def sent(copies):
     for copy in copies:
         copy.wait_send()
-
-
-SPLIT = 4
 
 
 class Gather:
@@ -108,7 +105,12 @@
         self.one_b = pl.ds(pl.multiple_of(half + 4 * piece + hi * (2 * piece) + bit * piece, 16), piece)
         self.two_a = pl.ds(pl.multiple_of(half + bit * (2 * piece), 16), 2 * piece)
         self.two_b = pl.ds(pl.multiple_of(half + 4 * piece + hi * (2 * piece), 16), 2 * piece)
-        self.half, self.step = half, 8 * piece // SPLIT
+        rows = lambda first, count: pl.ds(pl.multiple_of(half + first * piece, 16), count * piece)
+        self.pieces = (
+            (self.one_a, self.one_b),
+            (rows(bit * 2 + 1 - hi, 1), rows(4 + hi * 2 + 1 - bit, 1)),
+            (rows(2 - 2 * bit, 2), rows(6 - 2 * hi, 2)),
+        )
 
     def copies(self, stage, i):
         at, home, spot = self.at, self.home, self.spot
@@ -139,9 +141,17 @@
             return [same(6 + 2 * i, m, self.one_a, at["far"]), same(7 + 2 * i, m, self.one_b, at["side"])]
         if stage == 2:
             return [same(12 + 2 * i, m, self.two_a, at["side"]), same(13 + 2 * i, m, self.two_b, at["far"])]
+        raise ValueError(stage)
+
+    def to_twin(self, stage, i):
+        m, twin = self.chunks[i], self.at["twin"]
+        source = [self.spot.at[m, rows] for rows in self.pieces[stage]]
+        if stage == 0 and self.early is not None:
+            source = [self.early.at[i, p] for p in range(2)]
+        slot = 18 + 6 * i + 2 * stage
         return [
-            same(18 + SPLIT * i + n, m, pl.ds(pl.multiple_of(self.half + n * self.step, 16), self.step), at["twin"])
-            for n in range(SPLIT)
+            remote(src, self.spot.at[m, rows], self.send_sem.at[slot + n], self.recv_sem.at[slot + n], twin)
+            for n, (src, rows) in enumerate(zip(source, self.pieces[stage]))
         ]
 
     def start(self):
@@ -171,19 +181,22 @@
             arrive(self.copies(stage - 1, i))
             if stage == 1 and i == 1:
                 begin(self.copies(0, 2))
-            begin(self.copies(stage, i))
+            begin((self.copies(stage, i) if stage < 3 else []) + self.to_twin(stage - 1, i))
 
     def done(self, *parts):
         for i in parts:
-            arrive(self.copies(3, i))
+            for stage in range(3):
+                arrive(self.to_twin(stage, i))
 
     def sent(self):
-        for stage in range(0 if self.early is None else 1, 4):
+        for stage in range(3):
             for i in range(3):
-                sent(self.copies(stage, i))
-
-
-GATHER_SEMS = 18 + 3 * SPLIT
+                if stage > 0 or self.early is None:
+                    sent(self.copies(stage, i))
+                sent(self.to_twin(stage, i))
+
+
+GATHER_SEMS = 36
 PARTS = 2
 
 
@@ -494,11 +507,11 @@
 
 def ffn_kernel(
     classes, pairs, scatter,
-    xhat1_ref, rstd1_ref, gain_ref, shift_ref, wb_ref, wc_home, early_ref, vecs_ref, bdown_ref, cot_ref, own_ref,
+    xhat1_ref, rstd1_ref, gain_ref, shift_ref, wb_hbm, wc_home, early_ref, vecs_ref, bdown_ref, cot_hbm, own_ref,
     sw1_ref, sbias_ref, query_ref, w2_in, w3_in, b3_in,
     mixed_ref, gres_ref, dwb_ref, out_ref, hand_ref, pack_ref,
     w2_ref, w3_ref, b3_ref, gbup_ref, gvec_ref, gsw1_ref, act_ref, slope_ref, xhat2_ref, rstd2_ref,
-    stud_ref, dstud_ref, low_ref, flip_ref, wc_ref, dwc_ref, wsend, wrecv, msend, mrecv, local_sem, piece_sem, *parts,
+    stud_ref, dstud_ref, low_ref, flip_ref, wc_ref, dwc_ref, wsend, wrecv, msend, mrecv, local_sem, piece_sem, wb_ref, cot_ref, *parts,
 ):
     row_count, seq, dim = xhat1_ref.shape
     model_size = wb_ref.shape[0]
@@ -511,11 +524,16 @@
     own_pieces = gather.own_pieces(piece_sem)
     own_copy = pltpu.make_async_copy(wc_home, wc_ref.at[at["z"]], local_sem.at[0])
     own_copy.start()
+    loads = [
+        pltpu.make_async_copy(wb_hbm, wb_ref, local_sem.at[1]),
+        pltpu.make_async_copy(cot_hbm, cot_ref, local_sem.at[2]),
+    ]
+    begin(loads)
     for copy in own_pieces:
         copy.start()
     greet(at, 2 if scatter else 1, model_size)
     for i in (1, 0, 2):
-        begin(gather.copies(1, i))
+        begin(gather.copies(1, i) + gather.to_twin(0, i))
     if scatter:
         reducer = Reduce(at, model_size, dwc_ref, dwc_ref.at[:, :, at["lo"]], *parts, None, msend, mrecv)
 
@@ -546,6 +564,8 @@
     lax.fori_loop(0, blocks, prepare, 0)
     for copy in own_pieces:
         copy.wait()
+    loads[0].wait()
+
     def during(m, table):
         for when, actions in table.items():
             @pl.when(m == when)
@@ -608,6 +628,8 @@
     gvec_ref[...] = jnp.zeros_like(gvec_ref)
     gsw1_ref[...] = jnp.zeros_like(gsw1_ref)
     gbup_ref[...] = jnp.zeros_like(gbup_ref)
+
+    loads[1].wait()
 
     def norm_two_back(t, _):
         r, part = place(t)
@@ -727,7 +749,7 @@
     hbm = pl.BlockSpec(memory_space=pl.ANY)
     return pl.pallas_call(
         functools.partial(ffn_kernel, classes, pairs, scatter),
-        in_specs=[vmem] * 5 + [hbm, hbm] + [vmem] * 10,
+        in_specs=[vmem] * 4 + [hbm] * 3 + [vmem, vmem, hbm] + [vmem] * 7,
         out_specs=[vmem] * 6,
         out_shape=(
             jax.ShapeDtypeStruct((rows, seq, dim), BF16),
@@ -758,8 +780,10 @@
             dma((GATHER_SEMS,)),
             dma((REDUCE_SEMS,)),
             dma((REDUCE_SEMS,)),
-            dma((1,)),
+            dma((3,)),
             dma((6,)),
+            low(model_size, dim, inner),
+            low(rows, seq, dim),
             *(reduce_scratch(model_size, piece, inner) if scatter else ()),
         ],
         compiler_params=pltpu.CompilerParams(
@@ -1232,10 +1256,10 @@
 
 def leave_kernel(
     depth, pairs,
-    exit_ref, target_ref, tags_ref, own_ref, x_ref, gres_hbm, wa_ref, qkv_hbm, ctx_ref, lse_ref,
+    exit_ref, target_ref, tags_ref, own_ref, x_hbm, gres_hbm, wa_hbm, qkv_hbm, ctx_hbm, lse_ref,
     dwb_hbm, ownc_ref, hand_ref, pack_ref,
     rows_ref, mats_ref, sums_ref, bias_ref,
-    work_ref, acc_ref, mask_ref, p_ref, s_ref, xflip_ref, gflip_ref, dx_ref, dwa_ref,
+    x_ref, wa_ref, ctx_ref, work_ref, acc_ref, mask_ref, p_ref, s_ref, xflip_ref, gflip_ref, dx_ref, dwa_ref,
     own_half, *rest,
 ):
     parts_a, parts_b, parts_c, rest = rest[:7], rest[7:14], rest[14:19], rest[19:]
@@ -1328,6 +1352,9 @@
         return [
             pltpu.make_async_copy(qkv_hbm, work_ref, local_sem.at[2]),
             pltpu.make_async_copy(gres_hbm, acc_ref, local_sem.at[3]),
+            pltpu.make_async_copy(x_hbm, x_ref, local_sem.at[4]),
+            pltpu.make_async_copy(wa_hbm, wa_ref, local_sem.at[5]),
+            pltpu.make_async_copy(ctx_hbm, ctx_ref, local_sem.at[6]),
         ]
 
     def small_step(stage):
@@ -1369,13 +1396,13 @@
 
     steps = {
         0: [],
-        1: [(small_step, 0), (third.after_one,), (first.after_core, 0)],
-        2: [(first.after_core, 1), (first.after_one, 0)],
-        3: [(first.after_core, 2), (first.after_one, 1), (first.after_two, 0), (small_step, 1), (third.after_two,)],
-        4: [(first.after_core, 3), (first.after_one, 2), (first.after_two, 1), (small_step, 2)],
-        5: [(first.after_one, 3), (first.after_two, 2), (small_step, 3), (third.after_three,)],
-        6: [(second.after_core, 0), (first.after_two, 3), (small_step, 4)],
-        7: [(second.after_core, 1), (second.after_one, 0), (first.after_three,)],
+        1: [(small_step, 0), (third.after_one,)],
+        2: [],
+        3: [(first.after_core, 0), (small_step, 1), (third.after_two,)],
+        4: [(first.after_core, 1), (small_step, 2)],
+        5: [(first.after_one, 0), (small_step, 3), (third.after_three,)],
+        6: [(first.after_core, 2), (first.after_one, 1), (first.after_two, 0), (small_step, 4)],
+        7: [(first.after_core, 3), (first.after_one, 2), (first.after_two, 1), (second.after_core, 0)],
     }
 
     def weight_grads(i):
@@ -1446,7 +1473,8 @@
         for cut in range(CUTS):
             part = pl.ds(pl.multiple_of(z * token_part, 128), token_part)
             mine_refs[cut][z * row_count + r] = dx_ref[r, part, cut * wide : (cut + 1) * wide]
-    second.after_core(2)
+    first.after_one(3)
+    second.after_core(1)
     slots = slots_of_tags(tags_ref, depth, 2 * pairs, capacity)
 
     def give(cut):
@@ -1464,26 +1492,31 @@
         give(cut)
 
     returned(0)
+    first.after_two(2)
+    second.after_one(0)
+    second.after_core(2)
+    returned(1)
+    begin(bias_copies(0))
+    first.after_two(3)
     second.after_core(3)
     second.after_one(1)
+    returned(2)
     second.after_two(0)
-    begin(bias_copies(0))
-    returned(1)
-    second.after_one(2)
-    second.after_two(1)
-    first.after_four()
-    returned(2)
-    second.after_one(3)
-    second.after_two(2)
-    bias_step(0)
-    small_step(5)
     own_slots = pl.ds(b * depth, depth)
     back_got[own_slots] = back_ref[own_slots]
+    second.after_two(1)
+    second.after_one(2)
+    bias_step(0)
+    first.after_three()
+    second.after_two(2)
+    second.after_one(3)
     bias_step(1)
+    small_step(5)
+    first.after_four()
+    third.done()
     second.after_two(3)
+    bias_step(2)
     second.after_three()
-    bias_step(2)
-    third.done()
     bias_step(3)
     flat = slot_of_rows(exit_ref, target_ref, depth)
     for cut in range(CUTS):
@@ -1528,7 +1561,7 @@
     row_moves = CUTS * (rows * others + batch_size - 1)
     return pl.pallas_call(
         functools.partial(leave_kernel, depth, pairs),
-        in_specs=[smem, smem, vmem, vmem, vmem, hbm, vmem, hbm, vmem, vmem, hbm, vmem, vmem, vmem],
+        in_specs=[smem, smem, vmem, vmem, hbm, hbm, hbm, hbm, hbm, vmem, hbm, vmem, vmem, vmem],
         out_specs=[vmem, vmem, vmem, vmem],
         out_shape=(
             jax.ShapeDtypeStruct((row_total, token_part, dim), BF16),
@@ -1537,6 +1570,9 @@
             jax.ShapeDtypeStruct((8, 3 * group_dim), F32),
         ),
         scratch_shapes=[
+            low(rows, seq, dim),
+            low(model_size, dim, dim),
+            low(rows, model_size, group_dim, seq),
             low(rows, model_size, 3 * group_dim, seq),
             f32(rows, seq, dim),
             f32(seq, seq),
@@ -1570,7 +1606,7 @@
             dma((3 + others,)),
             dma((row_moves,)),
             dma((row_moves,)),
-            dma((4,)),
+            dma((7,)),
             *[low(capacity, token_part, dim // CUTS) for _ in range(CUTS)],
         ],
         compiler_params=pltpu.CompilerParams(

time: 292 us -> 285 us (0.976)
  Pallas kernels: 286 us -> 281 us
where the time goes in v2:
time: 285 us
  Pallas kernels  281 us (99%)
  local copies, waits for them, and re-layouts  2.98 us (1%)
    pallas_call x1, Pallas kernels, leave(): pl.pallas_call(functools.partial(leave_kernel, depth, pairs), in_specs=[s...  118 us
    pallas_call x1, Pallas kernels, enter(): pl.pallas_call(functools.partial(enter_kernel, depth, pairs), in_specs=[s...  83.5 us
    pallas_call x1, Pallas kernels, ffn_both(): pl.pallas_call(functools.partial(ffn_kernel, classes, pairs, scatter), in...  75.9 us

profile of v2, /device:TPU:1, one launch (start us, length us, event | category | flops | bytes accessed | tf_op | source)
XLA Modules:
  0.0 284.8 jit_solution(5735931668534165022)
XLA Ops:
  0.7 83.5 %enter.1 = (f32[8,640]{1,0:T(8,128)}, f32[2,8,640]{2,1,0:T(8,128)}, f32[4,8,768]{2,1,0:T(8,128)}, bf16[2,512,768]{2,1,0:T(8,128)(2,1)}, bf16[4,768,768]{2,1,0:T(...) custom-call(s32[7]{0:T(128)} %exit_ref.3, ...), custom_call_target="tpu_custom_call" | custom-call | tf_op jit(solution)/shard_map/enter/pallas_call | solution.py:1208
  84.1 75.9 %ffn_both.1 = (bf16[2,512,768]{2,1,0:T(8,128)(2,1)}, f32[2,512,768]{2,1,0:T(8,128)}, bf16[4,2,2,2,2,48,768]{6,5,4,3,2,1,0:T(8,128)(2,1)}, bf16[2,2,2,48,768]{4,3...) custom-call(f32[2,512,768]{2,1,0:T(8,128)} %get-tuple-element.56.xhat1_ref, ...), custom_call_target="tpu_custom_call" | custom-call | tf_op jit(solution)/shard_map/ffn_both/pallas_call | solution.py:750
  160.0 117.8 %leave.1 = (bf16[7,128,768]{2,1,0:T(8,128)(2,1)}, bf16[3,2,2,2,48,768]{5,4,3,2,1,0:T(8,128)(2,1)}, f32[2,4,128,128]{3,2,1,0:T(8,128)}, f32[8,576]{1,0:T(8,128)}) custom-call(s32[7]{0:T(128)} %exit_ref.3, s32[7]{0:T(128)} %target_ref.3, f32[2,8,640]{2,1,0:T(8,128)} %get-tuple-element.63.tags_ref, f32[8,640]{1,0:T(8,128)} %get-tuple-element.61.own_ref, ...), custom_call_target="tpu_custom_call" | custom-call | tf_op jit(solution)/shard_map/leave/pallas_call | solution.py:1562
  277.9 0.0 copy-start
  277.9 4.0 %finish.1 = (f32[3,192,384]{2,1,0:T(8,128)}, f32[2,96]{1,0:T(2,128)}, f32[192,384]{1,0:T(8,128)}, f32[768]{0:T(1024)}, f32[2,768]{1,0:T(2,128)}, /*index=5*/f32[...) custom-call(bf16[3,384,768]{2,1,0:T(8,128)(2,1)} %bitcast.9, ...), custom_call_target="tpu_custom_call" | custom-call | tf_op jit(solution)/shard_map/finish/pallas_call | solution.py:1671
  281.9 0.0 copy-done
  281.9 0.0 copy-start.1
  281.9 1.1 copy.43
  283.0 0.8 copy-done.1
  283.8 1.1 copy.44
Async XLA Ops:
  277.9 4.0 %copy-start = (bf16[2,512,768]{2,1,0:T(8,128)(2,1)S(1)}, bf16[2,512,768]{2,1,0:T(8,128)(2,1)}, u32[]{:S(2)}) copy-start(bf16[2,512,768]{2,1,0:T(8,128)(2,1)} %get-tuple-element.112) | copy-start | bytes 4718596
  281.9 1.9 copy-start.1

commit v3 on v2

--- a/solution.py
+++ b/solution.py
@@ -356,9 +356,8 @@
                 one(3, self.got_a.at[1 - b], self.got_a2, at["side"]),
                 one(4, self.got_b.at[1 - hi], self.got_b2, at["far"]),
             ]
-        if stage == 3:
-            return [one(5, self.out.at[lo, :, hi], self.out.at[lo, :, hi], at["far"])]
-        return [one(6, self.out.at[lo], self.out.at[lo], at["twin"])]
+        mine = self.out.at[lo, :, hi]
+        return [one(5 + n, mine, mine, at[peer]) for n, peer in enumerate(("far", "twin", "far_twin"))]
 
     def start(self):
         begin(self.copies(1) + self.copies(0))
@@ -380,15 +379,11 @@
             self.out[lo, p, hi] = total.astype(BF16)
         begin(self.copies(3))
 
-    def after_three(self):
+    def done(self):
         arrive(self.copies(3))
-        begin(self.copies(4))
-
-    def done(self):
-        arrive(self.copies(4))
 
     def sent(self):
-        for stage in range(5):
+        for stage in range(4):
             sent(self.copies(stage))
 
 
@@ -509,8 +504,8 @@
     classes, pairs, scatter,
     xhat1_ref, rstd1_ref, gain_ref, shift_ref, wb_hbm, wc_home, early_ref, vecs_ref, bdown_ref, cot_hbm, own_ref,
     sw1_ref, sbias_ref, query_ref, w2_in, w3_in, b3_in,
-    mixed_ref, gres_ref, dwb_ref, out_ref, hand_ref, pack_ref,
-    w2_ref, w3_ref, b3_ref, gbup_ref, gvec_ref, gsw1_ref, act_ref, slope_ref, xhat2_ref, rstd2_ref,
+    mixed_ref, gres_ref, dwb_ref, out_ref, hand_ref, packed_ref,
+    pack_ref, w2_ref, w3_ref, b3_ref, gbup_ref, gvec_ref, gsw1_ref, act_ref, slope_ref, xhat2_ref, rstd2_ref,
     stud_ref, dstud_ref, low_ref, flip_ref, wc_ref, dwc_ref, wsend, wrecv, msend, mrecv, local_sem, piece_sem, wb_ref, cot_ref, *parts,
 ):
     row_count, seq, dim = xhat1_ref.shape
@@ -723,6 +718,7 @@
             first = bup_at.start + j * 8
             pack_ref[first + model_size : first + 8] = jnp.zeros((8 - model_size, width), F32)
     pack_ref[bup_at.stop :] = jnp.zeros((pack_ref.shape[0] - bup_at.stop, width), F32)
+    packed_ref[...] = pack_ref[...].astype(BF16)
     if scatter:
         reducer.hand_over(out_ref, hand_ref)
         reducer.sent_early()
@@ -757,9 +753,10 @@
             jax.ShapeDtypeStruct(grid_shape, BF16),
             jax.ShapeDtypeStruct(grid_shape[1:2] + grid_shape[3:] if scatter else grid_shape, BF16),
             jax.ShapeDtypeStruct((2, PARTS, piece, inner), BF16),
-            jax.ShapeDtypeStruct((pack_rows(dim, width), width), F32),
+            jax.ShapeDtypeStruct((pack_rows(dim, width), width), BF16),
         ),
         scratch_shapes=[
+            f32(pack_rows(dim, width), width),
             f32(width, width),
             f32(width, width),
             f32(1, width),
@@ -1256,15 +1253,15 @@
 
 def leave_kernel(
     depth, pairs,
-    exit_ref, target_ref, tags_ref, own_ref, x_hbm, gres_hbm, wa_hbm, qkv_hbm, ctx_hbm, lse_ref,
+    tags_ref, own_ref, x_hbm, gres_hbm, wa_hbm, qkv_hbm, ctx_hbm, lse_ref,
     dwb_hbm, ownc_ref, hand_ref, pack_ref,
-    rows_ref, mats_ref, sums_ref, bias_ref,
+    back_got, mats_ref, sums_ref, bias_ref,
     x_ref, wa_ref, ctx_ref, work_ref, acc_ref, mask_ref, p_ref, s_ref, xflip_ref, gflip_ref, dx_ref, dwa_ref,
     own_half, *rest,
 ):
     parts_a, parts_b, parts_c, rest = rest[:7], rest[7:14], rest[14:19], rest[19:]
     (
-        small_acc, small_got, small_z, bias_acc, bias_got, bias_z, back_ref, back_got,
+        small_acc, small_got, small_z, bias_acc, bias_row, bias_got, bias_z, back_ref,
         msend, mrecv, ssend, srecv, bsend, brecv, rsend, rrecv, local_sem, *mine_refs,
     ) = rest
     row_count, seq, dim = x_ref.shape
@@ -1281,7 +1278,7 @@
     def shard(i):
         return {"mp": (z + i) % model_size}
 
-    first = Reduce(at, model_size, dwb_hbm, own_half, *parts_b, mats_ref.at[1], msend.at[1], mrecv.at[1])
+    first = Reduce(at, model_size, dwb_hbm, own_half, *parts_b, mats_ref.at[1], msend.at[1], mrecv.at[1], 0, True)
     second = Reduce(at, model_size, dwa_ref, dwa_ref.at[:, :, lo], *parts_a, mats_ref.at[0], msend.at[0], mrecv.at[0], 2, True)
     third = Finish(at, model_size, ownc_ref, hand_ref, *parts_c, mats_ref.at[2], msend.at[2], mrecv.at[2])
 
@@ -1310,11 +1307,8 @@
             return remote(src, dst, bsend.at[slot], brecv.at[slot], device)
 
         if stage < 3:
-            return [one(stage, bias_acc.at[stage], bias_got.at[stage], (twin, far, side)[stage])]
-        return [
-            one(2 + i, bias_acc.at[3, (z + i) % model_size], bias_z.at[i - 1], shard(i))
-            for i in range(1, model_size)
-        ]
+            return [one(stage, bias_row.at[stage], bias_got.at[stage], (twin, far, side)[stage])]
+        return [one(2 + i, bias_row.at[3], bias_z.at[i - 1], shard(i)) for i in range(1, model_size)]
 
     wide = dim // CUTS
 
@@ -1364,23 +1358,24 @@
         if stage in (1, 2):
             small_acc[stage] = small_acc[stage - 1] + small_got[stage]
         if stage == 3:
-            total = small_acc[2, z]
+            total = small_acc[2, z].astype(F32)
             for i in range(others):
-                total += small_z[i]
-            sums_ref[lo, z] = total
+                total += small_z[i].astype(F32)
+            sums_ref[lo, z] = total.astype(BF16)
         if stage < 5:
             begin(small_copies(stage + 1))
 
     def bias_step(stage):
         arrive(bias_copies(stage))
         if stage < 3:
-            bias_acc[stage + 1] = bias_acc[stage] + bias_got[stage]
+            bias_row[stage + 1] = bias_row[stage] + bias_got[stage]
             begin(bias_copies(stage + 1))
         else:
-            total = bias_acc[3, z]
+            total = bias_row[3]
             for i in range(others):
                 total += bias_z[i]
-            bias_ref[...] = total
+            own = sum(jnp.where(z == m, 1.0, 0.0) * total[m : m + 1] for m in range(model_size))
+            bias_ref[...] = jnp.broadcast_to(own, bias_ref.shape)
 
     begin(inputs())
     begin(local_copies())
@@ -1397,12 +1392,12 @@
     steps = {
         0: [],
         1: [(small_step, 0), (third.after_one,)],
-        2: [],
-        3: [(first.after_core, 0), (small_step, 1), (third.after_two,)],
-        4: [(first.after_core, 1), (small_step, 2)],
-        5: [(first.after_one, 0), (small_step, 3), (third.after_three,)],
-        6: [(first.after_core, 2), (first.after_one, 1), (first.after_two, 0), (small_step, 4)],
-        7: [(first.after_core, 3), (first.after_one, 2), (first.after_two, 1), (second.after_core, 0)],
+        2: [(first.after_core, 0)],
+        3: [(first.after_core, 1), (small_step, 1), (third.after_two,)],
+        4: [(first.after_one, 0), (small_step, 2)],
+        5: [(first.after_core, 2), (first.after_one, 1), (first.after_two, 0), (small_step, 3)],
+        6: [(first.after_core, 3), (first.after_two, 1), (small_step, 4)],
+        7: [(first.after_one, 2), (second.after_core, 0)],
     }
 
     def weight_grads(i):
@@ -1456,9 +1451,9 @@
             grads = work_ref[r, m]
             found = mm(jnp.ones((8, seq), BF16), grads, NT)
             if r == 0:
-                bias_acc[0, m] = found
+                bias_acc[m] = found
             else:
-                bias_acc[0, m] = bias_acc[0, m] + found
+                bias_acc[m] = bias_acc[m] + found
             acc_ref[r] = acc_ref[r] + mm(grads, wa_ref[m, : 3 * group_dim, :], TN)
             return 0
 
@@ -1496,6 +1491,9 @@
     second.after_one(0)
     second.after_core(2)
     returned(1)
+    bias_row[0] = jnp.zeros_like(bias_row[0])
+    for m in range(model_size):
+        bias_row[0, m : m + 1] = bias_acc[m, 0:1]
     begin(bias_copies(0))
     first.after_two(3)
     second.after_core(3)
@@ -1512,20 +1510,14 @@
     second.after_one(3)
     bias_step(1)
     small_step(5)
-    first.after_four()
     third.done()
     second.after_two(3)
     bias_step(2)
     second.after_three()
     bias_step(3)
-    flat = slot_of_rows(exit_ref, target_ref, depth)
     for cut in range(CUTS):
         arrive(batch_copies(cut))
 
-    for r in range(rows_ref.shape[0]):
-        k = jnp.minimum(jnp.maximum(flat[r], 0), batch_size * depth - 1)
-        alive = jnp.where(flat[r] >= 0, 1.0, 0.0)
-        rows_ref[r] = (back_got[k].astype(F32) * alive).astype(BF16)
     for reducer in (first, second):
         reducer.done()
         reducer.sent()
@@ -1540,7 +1532,7 @@
         sent(batch_copies(cut))
 
 
-def leave(exit_flag, target, tags, own, x, gres, w_a, qkv, ctx, lse, d_wb, mat_c, hand, pack, row_total, batch_size, pairs):
+def leave(tags, own, x, gres, w_a, qkv, ctx, lse, d_wb, mat_c, hand, pack, batch_size, pairs):
     rows, seq, dim = x.shape
     model_size = w_a.shape[0]
     group_dim = dim // model_size
@@ -1552,7 +1544,6 @@
     others = model_size - 1
     grid_shape = (model_size, 2, 2, PARTS, 2, piece, dim)
     pack_shape = (2, model_size, pack.shape[0] // (2 * model_size), pack.shape[1])
-    smem = pl.BlockSpec(memory_space=pltpu.SMEM)
     vmem = pl.BlockSpec(memory_space=pltpu.VMEM)
     hbm = pl.BlockSpec(memory_space=pl.ANY)
     dma = pltpu.SemaphoreType.DMA
@@ -1561,12 +1552,12 @@
     row_moves = CUTS * (rows * others + batch_size - 1)
     return pl.pallas_call(
         functools.partial(leave_kernel, depth, pairs),
-        in_specs=[smem, smem, vmem, vmem, hbm, hbm, hbm, hbm, hbm, vmem, hbm, vmem, vmem, vmem],
+        in_specs=[vmem, vmem, hbm, hbm, hbm, hbm, hbm, vmem, hbm, vmem, vmem, vmem],
         out_specs=[vmem, vmem, vmem, vmem],
         out_shape=(
-            jax.ShapeDtypeStruct((row_total, token_part, dim), BF16),
+            jax.ShapeDtypeStruct((slots, token_part, dim), BF16),
             jax.ShapeDtypeStruct((3,) + grid_shape[2:], BF16),
-            jax.ShapeDtypeStruct(pack_shape, F32),
+            jax.ShapeDtypeStruct(pack_shape, BF16),
             jax.ShapeDtypeStruct((8, 3 * group_dim), F32),
         ),
         scratch_shapes=[
@@ -1590,13 +1581,13 @@
             low(piece, dim),
             low(piece, dim),
             low(PARTS, piece, dim),
-            f32(3, *pack_shape[1:]),
-            f32(3, *pack_shape[1:]),
-            f32(others, *pack_shape[2:]),
-            f32(4, model_size, 8, 3 * group_dim),
-            f32(3, model_size, 8, 3 * group_dim),
+            low(3, *pack_shape[1:]),
+            low(3, *pack_shape[1:]),
+            low(others, *pack_shape[2:]),
+            f32(model_size, 8, 3 * group_dim),
+            f32(4, 8, 3 * group_dim),
+            f32(3, 8, 3 * group_dim),
             f32(others, 8, 3 * group_dim),
-            low(slots, token_part, dim),
             low(slots, token_part, dim),
             dma((3, REDUCE_SEMS)),
             dma((3, REDUCE_SEMS)),
@@ -1614,16 +1605,27 @@
         ),
         name="leave",
     )(
-        exit_flag, target, tags, own, x, gres, w_a, qkv, ctx, lse,
+        tags, own, x, gres, w_a, qkv, ctx, lse,
         d_wb.reshape(grid_shape), mat_c, hand, pack.reshape(pack_shape),
     )
 
 
 def finish_kernel(
-    classes, mats_ref, sums_ref, bias_ref,
-    gqkv_ref, gbqv_ref, gout_ref, gbout_ref, ggain_ref, gshift_ref, gup_ref, gbup_ref, gdown_ref, gbdown_ref,
-    gsw1_ref, gsbias_ref, gquery_ref, gsw2_ref, gsw3_ref, gsb3_ref,
+    classes, depth, mats_ref, low_ref, bias_ref, *rest
 ):
+    rows_in, rest = rest[: len(rest) - 18 + (1 if depth is None else 0)], rest[len(rest) - 18 + (1 if depth is None else 0) :]
+    (
+        gqkv_ref, gbqv_ref, gout_ref, gbout_ref, ggain_ref, gshift_ref, gup_ref, gbup_ref, gdown_ref, gbdown_ref,
+        gsw1_ref, gsbias_ref, gquery_ref, gsw2_ref, gsw3_ref, gsb3_ref, *rows_out, sums_ref,
+    ) = rest
+    if depth is not None:
+        exit_ref, target_ref, back_ref = rows_in
+        flat = slot_of_rows(exit_ref, target_ref, depth)
+        for r in range(rows_out[0].shape[0]):
+            k = jnp.minimum(jnp.maximum(flat[r], 0), back_ref.shape[0] - 1)
+            alive = jnp.where(flat[r] >= 0, 1.0, 0.0)
+            rows_out[0][r] = (back_ref[k].astype(F32) * alive).astype(BF16)
+    sums_ref[...] = low_ref[...].astype(F32)
     dim, width = gsw1_ref.shape
     group_dim = gout_ref.shape[0]
     b, z = lax.axis_index("batch"), lax.axis_index("mp")
@@ -1662,14 +1664,20 @@
     gsw3_ref[...] = sums_ref[w3_at][:classes]
 
 
-def finish(mats, sums, bias, model_size, classes):
+def finish(mats, sums, bias, model_size, classes, rows, slot_depth):
     depth, dim = mats.shape[1:]
     width = sums.shape[1]
     group_dim = dim // model_size
     batch_size = dim // depth
     f32 = lambda *shape: jax.ShapeDtypeStruct(shape, F32)
+    smem, vmem = pl.BlockSpec(memory_space=pltpu.SMEM), pl.BlockSpec(memory_space=pltpu.VMEM)
+    row_shapes = ()
+    if rows:
+        row_shapes = (jax.ShapeDtypeStruct((rows[0].shape[0],) + rows[2].shape[1:], BF16),)
     return pl.pallas_call(
-        functools.partial(finish_kernel, classes),
+        functools.partial(finish_kernel, classes, slot_depth if rows else None),
+        in_specs=[vmem] * 3 + ([smem, smem, vmem] if rows else []),
+        out_specs=[vmem] * (16 + len(row_shapes)),
         out_shape=(
             f32(3, group_dim, depth),
             f32(2, group_dim // batch_size),
@@ -1687,10 +1695,12 @@
             f32(width, width),
             f32(classes, width),
             f32(classes),
+            *row_shapes,
         ),
+        scratch_shapes=[pltpu.VMEM(sums.shape, F32)],
         compiler_params=pltpu.CompilerParams(vmem_limit_bytes=VMEM_MOST),
         name="finish",
-    )(mats, sums, bias)
+    )(mats, sums, bias, *rows)
 
 
 def rows_back(grad_x, exit_flag, target, live, slot_depth):
@@ -1753,9 +1763,9 @@
         s_w1, s_bias, s_query, s_w2, s_w3, s_b3,
     )
     if scatter:
-        grad_rows, mats, sums, bias_sum = leave(
-            exit_flag, target, got_tags, own, rows_own, grad_resid, w_a, qkv, ctx, lse, d_wb, mat_c, hand, pack,
-            row_count, batch_size, pair_count,
+        back, mats, sums, bias_sum = leave(
+            got_tags, own, rows_own, grad_resid, w_a, qkv, ctx, lse, d_wb, mat_c, hand, pack,
+            batch_size, pair_count,
         )
         mats = mats.reshape(3, model_dim // batch_size, model_dim)
         sums = sums.reshape(pack.shape)
@@ -1764,14 +1774,18 @@
         grad_rows = rows_back(grad_x, exit_flag, target, got_tags[:, :slot_depth, 2 * pair_count], slot_depth)
         whole = (model_size, model_dim, model_dim)
         mats = matrix_sums((d_wa, d_wb.reshape(whole), mat_c.reshape(whole)))
-        sums, bias_sum = lax.psum((pack, bias_part[:, 0]), ("grp", "batch", "mp"))
+        sums, bias_sum = lax.psum((pack.astype(F32), bias_part[:, 0]), ("grp", "batch", "mp"))
         bias_sum = lax.dynamic_index_in_dim(bias_sum, my_mp, 0)
         mats = jnp.stack(mats)
 
     (
         g_wqkv, g_bqv, g_wout, g_bout, g_gain, g_shift, g_wup, g_bup, g_wdown, g_bdown,
-        g_sw1, g_sbias, g_query, g_sw2, g_sw3, g_sb3,
-    ) = finish(mats, sums, bias_sum, model_size, s_w3.shape[1])
+        g_sw1, g_sbias, g_query, g_sw2, g_sw3, g_sb3, *rows_found,
+    ) = finish(
+        mats, sums, bias_sum, model_size, s_w3.shape[1], (exit_flag, target, back) if scatter else (), slot_depth
+    )
+    if scatter:
+        grad_rows = rows_found[0]
     return (
         mixed_out, grad_rows, jnp.transpose(g_wqkv, (0, 2, 1)), g_bqv, g_wout, g_bout, g_gain, g_shift, g_wup,
         g_bup, g_wdown, g_bdown, g_sw1, g_sbias, g_query, g_sw2, g_sw3.T, g_sb3,

time: 285 us -> 277 us (0.972)
  Pallas kernels: 281 us -> 275 us
    pallas_call x2, Pallas kernels: 122 us -> 116 us  [the longest x1 111 us: leave(): pl.pallas_call(functools.partial(leave_kernel, depth, pairs), in_specs=[v...]
where the time goes in v3:
time: 277 us
  Pallas kernels  275 us (99%)
    pallas_call x1, Pallas kernels, leave(): pl.pallas_call(functools.partial(leave_kernel, depth, pairs), in_specs=[v...  111 us
    pallas_call x1, Pallas kernels, enter(): pl.pallas_call(functools.partial(enter_kernel, depth, pairs), in_specs=[s...  83.5 us
    pallas_call x1, Pallas kernels, ffn_both(): pl.pallas_call(functools.partial(ffn_kernel, classes, pairs, scatter), in...  75.8 us

profile of v3, /device:TPU:1, one launch (start us, length us, event | category | flops | bytes accessed | tf_op | source)
XLA Modules:
  0.0 277.2 jit_solution(16754253421348075970)
XLA Ops:
  0.7 83.5 %enter.1 = (f32[8,640]{1,0:T(8,128)}, f32[2,8,640]{2,1,0:T(8,128)}, f32[4,8,768]{2,1,0:T(8,128)}, bf16[2,512,768]{2,1,0:T(8,128)(2,1)}, bf16[4,768,768]{2,1,0:T(...) custom-call(s32[7]{0:T(128)} %rest_0_.1, ...), custom_call_target="tpu_custom_call" | custom-call | tf_op jit(solution)/shard_map/enter/pallas_call | solution.py:1205
  84.1 75.8 %ffn_both.1 = (bf16[2,512,768]{2,1,0:T(8,128)(2,1)}, f32[2,512,768]{2,1,0:T(8,128)}, bf16[4,2,2,2,2,48,768]{6,5,4,3,2,1,0:T(8,128)(2,1)}, bf16[2,2,2,48,768]{4,3...) custom-call(f32[2,512,768]{2,1,0:T(8,128)} %get-tuple-element.57.xhat1_ref, ...), custom_call_target="tpu_custom_call" | custom-call | tf_op jit(solution)/shard_map/ffn_both/pallas_call | solution.py:746
  160.0 111.2 %leave.1 = (bf16[8,128,768]{2,1,0:T(8,128)(2,1)}, bf16[3,2,2,2,48,768]{5,4,3,2,1,0:T(8,128)(2,1)}, bf16[2,4,128,128]{3,2,1,0:T(8,128)(2,1)}, f32[8,576]{1,0:T(8,128)}) custom-call(f32[2,8,640]{2,1,0:T(8,128)} %get-tuple-element.64.tags_ref, f32[8,640]{1,0:T(8,128)} %get-tuple-element.62.own_ref, bf16[2,512,768]{2,1,0:T(8,128)(2,1)} %get-tuple-element.65.x_hbm, ...), custom_call_target="tpu_custom_call" | custom-call | tf_op jit(solution)/shard_map/leave/pallas_call | solution.py:1553
  271.1 0.0 copy-start
  271.2 4.9 %finish.1 = (f32[3,192,384]{2,1,0:T(8,128)}, f32[2,96]{1,0:T(2,128)}, f32[192,384]{1,0:T(8,128)}, f32[768]{0:T(1024)}, f32[2,768]{1,0:T(2,128)}, /*index=5*/f32[...) custom-call(bf16[3,384,768]{2,1,0:T(8,128)(2,1)} %bitcast.9, ...), custom_call_target="tpu_custom_call" | custom-call | tf_op jit(solution)/shard_map/finish/pallas_call | solution.py:1677
  276.1 0.0 copy-done
  276.1 1.1 copy.42
Async XLA Ops:
  271.1 4.9 %copy-start = (bf16[2,512,768]{2,1,0:T(8,128)(2,1)S(1)}, bf16[2,512,768]{2,1,0:T(8,128)(2,1)}, u32[]{:S(2)}) copy-start(bf16[2,512,768]{2,1,0:T(8,128)(2,1)} %get-tuple-element.114) | copy-start | bytes 4718596

commit v4 on v3

--- a/solution.py
+++ b/solution.py
@@ -356,8 +356,9 @@
                 one(3, self.got_a.at[1 - b], self.got_a2, at["side"]),
                 one(4, self.got_b.at[1 - hi], self.got_b2, at["far"]),
             ]
-        mine = self.out.at[lo, :, hi]
-        return [one(5 + n, mine, mine, at[peer]) for n, peer in enumerate(("far", "twin", "far_twin"))]
+        if stage == 3:
+            return [one(5, self.out.at[lo, :, hi], self.out.at[lo, :, hi], at["far"])]
+        return [one(6, self.out.at[lo], self.out.at[lo], at["twin"])]
 
     def start(self):
         begin(self.copies(1) + self.copies(0))
@@ -379,11 +380,15 @@
             self.out[lo, p, hi] = total.astype(BF16)
         begin(self.copies(3))
 
+    def after_three(self):
+        arrive(self.copies(3))
+        begin(self.copies(4))
+
     def done(self):
-        arrive(self.copies(3))
+        arrive(self.copies(4))
 
     def sent(self):
-        for stage in range(4):
+        for stage in range(5):
             sent(self.copies(stage))
 
 
@@ -794,7 +799,7 @@
 
 
 TILE_Q = 256
-TILE_BACK = 64
+TILE_BACK = 128
 
 
 def backward_group(grad_ctx, ctx_of, load, store, mask, lse_of, group_dim, p_ref, s_ref):
@@ -1279,7 +1284,7 @@
         return {"mp": (z + i) % model_size}
 
     first = Reduce(at, model_size, dwb_hbm, own_half, *parts_b, mats_ref.at[1], msend.at[1], mrecv.at[1], 0, True)
-    second = Reduce(at, model_size, dwa_ref, dwa_ref.at[:, :, lo], *parts_a, mats_ref.at[0], msend.at[0], mrecv.at[0], 2, True)
+    second = Reduce(at, model_size, dwa_ref, dwa_ref.at[:, :, lo], *parts_a, mats_ref.at[0], msend.at[0], mrecv.at[0], 3, True)
     third = Finish(at, model_size, ownc_ref, hand_ref, *parts_c, mats_ref.at[2], msend.at[2], mrecv.at[2])
 
     def small_copies(stage):
@@ -1395,7 +1400,7 @@
         2: [(first.after_core, 0)],
         3: [(first.after_core, 1), (small_step, 1), (third.after_two,)],
         4: [(first.after_one, 0), (small_step, 2)],
-        5: [(first.after_core, 2), (first.after_one, 1), (first.after_two, 0), (small_step, 3)],
+        5: [(first.after_core, 2), (first.after_one, 1), (first.after_two, 0), (small_step, 3), (third.after_three,)],
         6: [(first.after_core, 3), (first.after_two, 1), (small_step, 4)],
         7: [(first.after_one, 2), (second.after_core, 0)],
     }

time: 277 us -> 276 us (level)
  Pallas kernels: 275 us -> 272 us
    pallas_call x1, Pallas kernels: 111 us -> 108 us  [leave(): pl.pallas_call(functools.partial(leave_kernel, depth, pairs), in_specs=[v...]
where the time goes in v4:
time: 276 us; the launch traced here: 274 us
  Pallas kernels  272 us (99%)
    pallas_call x1, Pallas kernels, leave(): pl.pallas_call(functools.partial(leave_kernel, depth, pairs), in_specs=[v...  108 us
    pallas_call x1, Pallas kernels, enter(): pl.pallas_call(functools.partial(enter_kernel, depth, pairs), in_specs=[s...  83.5 us
    pallas_call x1, Pallas kernels, ffn_both(): pl.pallas_call(functools.partial(ffn_kernel, classes, pairs, scatter), in...  75.8 us

profile of v4, /device:TPU:1, one launch (start us, length us, event | category | flops | bytes accessed | tf_op | source)
XLA Modules:
  0.0 274.1 jit_solution(10973599394951438818)
XLA Ops:
  0.7 83.5 %enter.1 = (f32[8,640]{1,0:T(8,128)}, f32[2,8,640]{2,1,0:T(8,128)}, f32[4,8,768]{2,1,0:T(8,128)}, bf16[2,512,768]{2,1,0:T(8,128)(2,1)}, bf16[4,768,768]{2,1,0:T(...) custom-call(s32[7]{0:T(128)} %rest_0_.1, ...), custom_call_target="tpu_custom_call" | custom-call | tf_op jit(solution)/shard_map/enter/pallas_call | solution.py:1210
  84.1 75.8 %ffn_both.1 = (bf16[2,512,768]{2,1,0:T(8,128)(2,1)}, f32[2,512,768]{2,1,0:T(8,128)}, bf16[4,2,2,2,2,48,768]{6,5,4,3,2,1,0:T(8,128)(2,1)}, bf16[2,2,2,48,768]{4,3...) custom-call(f32[2,512,768]{2,1,0:T(8,128)} %get-tuple-element.57.xhat1_ref, ...), custom_call_target="tpu_custom_call" | custom-call | tf_op jit(solution)/shard_map/ffn_both/pallas_call | solution.py:751
  160.0 108.0 %leave.1 = (bf16[8,128,768]{2,1,0:T(8,128)(2,1)}, bf16[3,2,2,2,48,768]{5,4,3,2,1,0:T(8,128)(2,1)}, bf16[2,4,128,128]{3,2,1,0:T(8,128)(2,1)}, f32[8,576]{1,0:T(8,128)}) custom-call(f32[2,8,640]{2,1,0:T(8,128)} %get-tuple-element.64.tags_ref, f32[8,640]{1,0:T(8,128)} %get-tuple-element.62.own_ref, bf16[2,512,768]{2,1,0:T(8,128)(2,1)} %get-tuple-element.65.x_hbm, ...), custom_call_target="tpu_custom_call" | custom-call | tf_op jit(solution)/shard_map/leave/pallas_call | solution.py:1558
  268.0 0.0 copy-start
  268.0 4.9 %finish.1 = (f32[3,192,384]{2,1,0:T(8,128)}, f32[2,96]{1,0:T(2,128)}, f32[192,384]{1,0:T(8,128)}, f32[768]{0:T(1024)}, f32[2,768]{1,0:T(2,128)}, /*index=5*/f32[...) custom-call(bf16[3,384,768]{2,1,0:T(8,128)(2,1)} %bitcast.9, ...), custom_call_target="tpu_custom_call" | custom-call | tf_op jit(solution)/shard_map/finish/pallas_call | solution.py:1682
  272.9 0.0 copy-done
  272.9 1.1 copy.42
Async XLA Ops:
  268.0 4.9 %copy-start = (bf16[2,512,768]{2,1,0:T(8,128)(2,1)S(1)}, bf16[2,512,768]{2,1,0:T(8,128)(2,1)}, u32[]{:S(2)}) copy-start(bf16[2,512,768]{2,1,0:T(8,128)(2,1)} %get-tuple-element.114) | copy-start | bytes 4718596
